TPU v7x, 32 devices: a whole 2x2x4 slice. The times are simulated.
32 devices in a mesh: slide: 2 (over y), seq: 4 (over z), head: 2 (over x), rep: 2 (over core).
Axes of the slice: x: 2, y: 2, z: 4, core: 2. Of those that a mesh axis runs over, the one named last changes fastest.
Arguments:
- tiles: bfloat16 [16384, 768], P(('slide', 'seq', 'rep')), parts along dimension 0, may hold values from -6 to 6
- labels: int32 [16384], P(('slide', 'seq', 'rep')), parts along dimension 0, may hold values from 0 to 7
- counts: int32 [16], P(('slide', 'seq', 'rep')), parts along dimension 0, may hold values from 256 to 1024, as said below
- offsets: int32 [2, 2], P(None, 'head'), may hold values from 0 to 1, as said below
- w_query: bfloat16 [768, 128], P(None, 'head'), may hold values from -0.21875 to 0.21875
- w_key: bfloat16 [768, 128], P(None, 'head'), may hold values from -0.21875 to 0.21875
- w_value: bfloat16 [768, 128], P(None, 'head'), may hold values from -0.21875 to 0.21875
- w_out: bfloat16 [128, 768], P('head'), may hold values from -2 to 2
- ln_gain: float32 [768], replicated, may hold values from 0.5 to 1.5
- w_class: bfloat16 [768, 8], replicated, may hold values from -0.875 to 0.875
Outputs:
- tile_loss: float32 [2], P('slide'), parts along dimension 0
- grad_query: float32 [1536, 128], P('slide', 'head'), parts along dimension 0
- grad_key: float32 [1536, 128], P('slide', 'head'), parts along dimension 0
- grad_value: float32 [1536, 128], P('slide', 'head'), parts along dimension 0
- grad_out: float32 [128, 1536], P('head', 'slide'), parts along dimension 1
There are 2 independent parts, one for each index of `slide`. A program takes and returns all parts, laid end to end along the dimension named above; an argument that names none is the same for every part. Nothing has to cross between parts.
Inputs may be any that keep to these rules, and one draw needn't show every extreme that they name: `counts`: valid tiles of each device's slots; some device of every slide holds 1024. `offsets`: row 0 is below 2 and takes every value below it over the heads; row 1 is distinct over the heads.
All inputs are finite; a program needn't handle non-finite values.
Results may differ from a plain program's by a relative error of at most 0.017.
Values may be sent and summed in bfloat16 or wider, within the bound.
A program may use at most 128 MiB of HBM per device.

v0:
```python
import math

import jax
import jax.numpy as jnp
from jax import lax
from jax.sharding import PartitionSpec as P


def lookup(table, index):
    hits = index[..., None] == jnp.arange(table.shape[0], dtype=jnp.int32)
    return jnp.sum(jnp.where(hits, table, 0), axis=-1)


def select(source, offset, stride):
    shaped = source.reshape((source.shape[0] // stride, stride) + source.shape[1:])
    return lax.dynamic_index_in_dim(shaped, offset, axis=1, keepdims=False)


def spread(values, offset, stride, filler):
    chosen = (jnp.arange(stride) == offset).reshape((1, stride) + (1,) * (values.ndim - 1))
    placed = jnp.where(chosen, jnp.expand_dims(values, 1), filler)
    return placed.reshape((values.shape[0] * stride,) + values.shape[1:])


def masked_scores(rows_query, rows_key, key_ok, factor):
    raw = (
        lax.dot_general(
            rows_query, rows_key, (((1,), (1,)), ((), ())), preferred_element_type=jnp.float32
        )
        * factor
    )
    return jnp.where(key_ok[None, :], raw, -jnp.inf)


def contract_rows(left, right):
    return lax.dot_general(
        left, right, (((0,), (0,)), ((), ())), preferred_element_type=jnp.float32
    )


def contract_cols(left, right):
    return lax.dot_general(
        left, right, (((1,), (1,)), ((), ())), preferred_element_type=jnp.float32
    )


def body(tiles, labels, counts, offsets, w_query, w_key, w_value, w_out, ln_gain, w_class):
    tile_rows = tiles.shape[0]
    head_size = w_query.shape[1]
    factor = 1.0 / math.sqrt(head_size)
    shards = lax.axis_size(("seq", "rep"))
    pair_stride = lax.axis_size("rep")
    far_stride = shards // 4
    far_rows = tile_rows // far_stride
    pair_base = lax.axis_index(("seq", "rep")) - lax.axis_index("rep")
    partner_offset = offsets[0, 0]
    distant_offset = offsets[1, 0]
    counts_all = lax.all_gather(counts, ("seq", "rep"), axis=0, tiled=True)
    position = jnp.arange(tile_rows, dtype=jnp.int32)
    own_ok = position < counts[0]
    queries = jnp.dot(tiles, w_query, preferred_element_type=jnp.float32).astype(jnp.bfloat16)
    keys = jnp.dot(tiles, w_key, preferred_element_type=jnp.float32).astype(jnp.bfloat16)
    values = jnp.dot(tiles, w_value, preferred_element_type=jnp.float32).astype(jnp.bfloat16)
    pair_key, pair_value = (
        lax.all_gather(select(keys, partner_offset, pair_stride), "rep", axis=0, tiled=True),
        lax.all_gather(select(values, partner_offset, pair_stride), "rep", axis=0, tiled=True),
    )
    far_key, far_value = (
        lax.all_gather(
            select(keys, distant_offset, far_stride), ("seq", "rep"), axis=0, tiled=True
        ),
        lax.all_gather(
            select(values, distant_offset, far_stride), ("seq", "rep"), axis=0, tiled=True
        ),
    )
    pair_slot = jnp.arange(tile_rows // pair_stride, dtype=jnp.int32)
    pair_owner = pair_base + jnp.arange(pair_stride, dtype=jnp.int32)[:, None]
    pair_ok = (
        pair_slot[None, :] * pair_stride + partner_offset < lookup(counts_all, pair_owner)
    ).reshape(tile_rows)
    far_slot = jnp.arange(shards * far_rows, dtype=jnp.int32)
    far_ok = far_slot % far_rows * far_stride + distant_offset < lookup(
        counts_all, far_slot // far_rows
    )
    rates = (
        (queries, keys, values, own_ok, 0, 1),
        (
            select(queries, partner_offset, pair_stride),
            pair_key,
            pair_value,
            pair_ok,
            partner_offset,
            pair_stride,
        ),
        (
            select(queries, distant_offset, far_stride),
            far_key,
            far_value,
            far_ok,
            distant_offset,
            far_stride,
        ),
    )
    scores = [masked_scores(member[0], member[1], member[3], factor) for member in rates]
    row_top = jnp.full((tile_rows,), -jnp.inf, jnp.float32)
    for member, block in zip(rates, scores):
        row_top = jnp.maximum(
            row_top, spread(jnp.max(block, axis=-1), member[4], member[5], -jnp.inf)
        )
    row_total = jnp.zeros((tile_rows,), jnp.float32)
    weighted = jnp.zeros((tile_rows, head_size), jnp.float32)
    exponents = []
    for member, block in zip(rates, scores):
        expo = jnp.exp(block - select(row_top, member[4], member[5])[:, None])
        exponents.append(expo)
        row_total = row_total + spread(jnp.sum(expo, axis=-1), member[4], member[5], 0.0)
        summed = jnp.dot(expo.astype(jnp.bfloat16), member[2], preferred_element_type=jnp.float32)
        weighted = weighted + spread(summed, member[4], member[5], 0.0)
    attended = (weighted / row_total[:, None]).astype(jnp.bfloat16)
    partial_mix = jnp.dot(attended, w_out, preferred_element_type=jnp.float32)
    mixed = tiles.astype(jnp.float32) + lax.psum(partial_mix.astype(jnp.bfloat16), "head").astype(
        jnp.float32
    )
    center = mixed - jnp.mean(mixed, axis=-1, keepdims=True)
    inv_dev = lax.rsqrt(jnp.mean(center * center, axis=-1, keepdims=True) + 1e-05)
    normal = center * inv_dev
    normed = (normal * ln_gain).astype(jnp.bfloat16)
    logits = jnp.dot(normed, w_class, preferred_element_type=jnp.float32)
    peak = jnp.max(logits, axis=-1, keepdims=True)
    log_total = jnp.log(jnp.sum(jnp.exp(logits - peak), axis=-1, keepdims=True)) + peak
    onehot = (labels[:, None] == jnp.arange(w_class.shape[1], dtype=jnp.int32)[None, :]).astype(
        jnp.float32
    )
    cross = log_total[:, 0] - jnp.sum(onehot * logits, axis=-1)
    loss_part = jnp.sum(jnp.where(own_ok, cross, 0.0)) / tile_rows
    grad_logits = (
        (jnp.exp(logits - log_total) - onehot) * own_ok[:, None].astype(jnp.float32) / tile_rows
    )
    grad_normed = jnp.dot(
        grad_logits, w_class.astype(jnp.float32).T, precision=lax.Precision.HIGHEST
    )
    grad_normal = grad_normed * ln_gain
    grad_mixed = inv_dev * (
        grad_normal
        - jnp.mean(grad_normal, axis=-1, keepdims=True)
        - normal * jnp.mean(grad_normal * normal, axis=-1, keepdims=True)
    )
    grad_mixed = grad_mixed.astype(jnp.bfloat16)
    grad_out = contract_rows(attended, grad_mixed)
    grad_attended = contract_cols(grad_mixed, w_out).astype(jnp.bfloat16)
    delta = jnp.sum(grad_attended.astype(jnp.float32) * attended.astype(jnp.float32), axis=-1)
    grad_rows_query = jnp.zeros((tile_rows, head_size), jnp.float32)
    key_terms = []
    for number, member in enumerate(rates):
        prob = exponents[number] / select(row_total, member[4], member[5])[:, None]
        sub_grad = select(grad_attended, member[4], member[5])
        dprob = contract_cols(sub_grad, member[2])
        dscore = (prob * (dprob - select(delta, member[4], member[5])[:, None])).astype(
            jnp.bfloat16
        )
        grad_rows_query = grad_rows_query + spread(
            jnp.dot(dscore, member[1], preferred_element_type=jnp.float32) * factor,
            member[4],
            member[5],
            0.0,
        )
        key_terms.append(
            (
                contract_rows(dscore, member[0]) * factor,
                contract_rows(prob.astype(jnp.bfloat16), sub_grad),
            )
        )
    pair_dk, pair_dv = (
        lax.psum_scatter(
            key_terms[1][0].astype(jnp.bfloat16), "rep", scatter_dimension=0, tiled=True
        ).astype(jnp.float32),
        lax.psum_scatter(
            key_terms[1][1].astype(jnp.bfloat16), "rep", scatter_dimension=0, tiled=True
        ).astype(jnp.float32),
    )
    far_dk, far_dv = (
        lax.psum_scatter(
            key_terms[2][0].astype(jnp.bfloat16), ("seq", "rep"), scatter_dimension=0, tiled=True
        ).astype(jnp.float32),
        lax.psum_scatter(
            key_terms[2][1].astype(jnp.bfloat16), ("seq", "rep"), scatter_dimension=0, tiled=True
        ).astype(jnp.float32),
    )
    grad_keys = (
        key_terms[0][0]
        + spread(pair_dk, partner_offset, pair_stride, 0.0)
        + spread(far_dk, distant_offset, far_stride, 0.0)
    )
    grad_values = (
        key_terms[0][1]
        + spread(pair_dv, partner_offset, pair_stride, 0.0)
        + spread(far_dv, distant_offset, far_stride, 0.0)
    )
    grad_query = contract_rows(tiles, grad_rows_query.astype(jnp.bfloat16))
    grad_key = contract_rows(tiles, grad_keys.astype(jnp.bfloat16))
    grad_value = contract_rows(tiles, grad_values.astype(jnp.bfloat16))
    totals = (
        lax.psum(grad_query.astype(jnp.bfloat16), ("seq", "rep")).astype(jnp.float32),
        lax.psum(grad_key.astype(jnp.bfloat16), ("seq", "rep")).astype(jnp.float32),
        lax.psum(grad_value.astype(jnp.bfloat16), ("seq", "rep")).astype(jnp.float32),
        lax.psum(grad_out.astype(jnp.bfloat16), ("seq", "rep")).astype(jnp.float32),
        lax.psum(loss_part.reshape(1).astype(jnp.bfloat16), ("seq", "rep")).astype(jnp.float32),
    )
    return (totals[4], totals[0], totals[1], totals[2], totals[3])


def solution(mesh):
    placed = (
        P(("slide", "seq", "rep"), None),
        P(("slide", "seq", "rep")),
        P(("slide", "seq", "rep")),
        P(None, "head"),
        P(None, "head"),
        P(None, "head"),
        P(None, "head"),
        P("head", None),
        P(),
        P(),
    )
    return jax.shard_map(
        body,
        mesh=mesh,
        in_specs=placed,
        out_specs=(
            P("slide"),
            P("slide", "head"),
            P("slide", "head"),
            P("slide", "head"),
            P("head", "slide"),
        ),
        check_vma=False,
    )
```

profile of v0, /device:TPU:0, one launch (start us, length us, event | category | flops | bytes accessed | tf_op | source)
XLA Modules:
  0.0 353.2 jit_solution(15146557121422730132)
XLA Ops:
  7.3 1.4 fusion.137
  9.9 1.3 iota_compare_fusion.4
  13.2 1.2 dynamic-slice.4
  15.9 10.6 %all-reduce = s32[8]{0:T(128)S(1)} all-reduce(s32[8]{0:T(128)S(1)} %dynamic-update-slice), channel_id=1, replica_groups=mesh['slide'=2,'seq'=4,'head'=2,'rep'=2] {'seq','rep'}, use_global_device_ids=true, to_apply=%add | all-reduce | flops 8 | bytes 64
  28.0 2.0 convolution_convert_fusion.6
  30.0 2.1 convolution_convert_fusion.5
  37.0 1.1 constant_dynamic-slice_fusion.3
  38.2 1.9 all-gather.2
  40.5 1.9 all-gather
  42.4 14.8 %all-gather.1 = bf16[4096,1,64]{0,2,1:T(8,128)(2,1)S(1)} all-gather(bf16[512,1,64]{0,2,1:T(8,128)(2,1)S(1)} %copy.82), channel_id=3, replica_groups=mesh['slide'=2,'seq'=4,'head'=2,'rep'=2] {'seq','rep'}, dimensions={0}, use_global_device_ids=true | all-gather | bytes 589824 | tf_op jit(solution)/shard_map/all_gather | solution.py:69
  57.2 16.0 %all-gather.3 = bf16[4096,1,64]{0,2,1:T(8,128)(2,1)} all-gather(bf16[512,1,64]{0,2,1:T(8,128)(2,1)S(1)} %copy.87), channel_id=5, replica_groups=mesh['slide'=2,'seq'=4,'head'=2,'rep'=2] {'seq','rep'}, dimensions={0}, use_global_device_ids=true | all-gather | bytes 589824 | tf_op jit(solution)/shard_map/all_gather | solution.py:72
  73.2 2.7 fusion.21
  76.2 2.8 fusion.9
  79.2 4.5 %fusion = (f32[512]{0:T(512)S(1)}, f32[512,4096]{1,0:T(8,128)}) fusion(pred[4096]{0:T(1024)(128)(4,1)S(1)} %fusion.109, bf16[4096,1,64]{0,2,1:T(8,128)(2,1)S(1)} %all-gather.1, bf16[512,1,64]{0,2,1:T(8,128)(2,1)S(1)} %copy-done.18), kind=kOutput, calls=%fused_computation.3 | convolution fusion | flops 274726400 | bytes 8984576 | tf_op jit(solution)/shard_map/dot_general | solution.py:27
  84.6 2.1 fusion.53
  87.0 4.5 %fusion.3 = f32[512]{0:T(512)S(1)} fusion(f32[512,4096]{1,0:T(8,128)} %get-tuple-element.32, f32[512]{0:T(512)S(1)} %get-tuple-element.12, pred[4096]{0:T(1024)(128)(4,1)S(1)} %fusion.109), kind=kLoop, calls=%fused_computation.8 | loop fusion | flops 8388096 | bytes 8396800 | tf_op jit(solution)/shard_map/reduce_sum | solution.py:116
  91.9 2.2 fusion.62
  94.4 5.1 %fusion.6 = f32[512,64]{1,0:T(8,128)S(1)} fusion(f32[512,4096]{1,0:T(8,128)} %get-tuple-element.32, f32[512]{0:T(512)S(1)} %get-tuple-element.12, pred[4096]{0:T(1024)(128)(4,1)S(1)} %fusion.109, bf16[4096,1,64]{0,2,1:T(8,128)(2,1)S(1)} %copy-done.24), kind=kOutput, calls=%fused_computation.14 | convolution fusion | flops 276824064 | bytes 9050112 | tf_op jit(solution)/shard_map/dot_general | solution.py:117
  99.9 3.2 fusion.14
  103.3 1.1 fusion.58
  104.5 1.8 convolution_convert_fusion.1
  107.4 49.1 %all-reduce.5.cloned.1.call-done = bf16[1024,768]{1,0:T(8,128)(2,1)} async-done(((bf16[1024,768]{1,0:T(8,128)(2,1)}), bf16[1024,768]{1,0:T(8,128)(2,1)}) %all-reduce.5.cloned.1.call-update) | async-done | bytes 1572880 | tf_op jit(solution)/shard_map/psum | solution.py:121
  156.5 2.0 fusion.11
  158.5 0.8 multiply_reduce_fusion.1
  159.3 0.9 fusion.138
  161.0 2.4 multiply_reduce_fusion.2
  163.4 1.4 multiply_convert_fusion.2
  164.8 1.3 multiply_reduce_fusion.3
  166.2 1.0 dynamic-slice_reduce_fusion.2
  167.2 1.1 copy.92
  168.3 1.3 constant_dynamic-slice_fusion.1
  169.6 1.1 copy.93
  170.7 2.9 convolution_convert_fusion.2
  173.6 2.5 multiply_convert_fusion.4
  176.2 1.1 convolution_multiply_fusion.5
  177.3 1.0 fusion.44
  179.3 1.0 copy.94
  180.3 1.0 broadcast_in_dim.325
  181.3 1.9 copy.95
  183.3 6.4 %multiply_convert_fusion = bf16[512,4096]{1,0:T(8,128)(2,1)S(1)} fusion(f32[512]{0:T(512)S(1)} %copy-done.32, bf16[4096,1,64]{0,2,1:T(8,128)(2,1)} %all-gather.3, bf16[512,1,64]{0,2,1:T(8,128)(2,1)} %copy.96, f32[512]{0:T(512)S(1)} %get-tuple-element.8, f32[512]{0:T(512)S(1)} %get-tuple-element.12, f32[512,4096]{1,0:T(8,128)} %get-tuple-element.32, ...), kind=kOutput, calls=%fused_computation | convolution fusion | flops 283115520 | bytes 13182976 | tf_op jit(solution)/shard_map/dot_general | solution.py:42
  189.7 1.9 copy-done.2
  191.6 1.4 convolution_multiply_fusion.4
  193.0 0.8 copy.97
  193.9 2.0 broadcast_in_dim.327
  195.8 1.9 copy.98
  197.8 3.9 %fusion.1 = bf16[4096,64]{0,1:T(8,128)(2,1)} fusion(bf16[512,4096]{1,0:T(8,128)(2,1)} %copy-done.2, bf16[512,1,64]{0,2,1:T(8,128)(2,1)S(1)} %copy-done.19), kind=kOutput, calls=%fused_computation.6 | convolution fusion | flops 268959744 | bytes 4784128 | tf_op jit(solution)/shard_map/dot_general | solution.py:36
  201.7 1.0 convolution_convert_fusion.7
  202.8 5.6 %convolution_convert_fusion = bf16[4096,64]{0,1:T(8,128)(2,1)} fusion(bf16[512,1,64]{0,2,1:T(8,128)(2,1)S(1)} %copy-done.28, f32[512,4096]{1,0:T(8,128)} %get-tuple-element.32, f32[512]{0:T(512)S(1)} %get-tuple-element.8, f32[512]{0:T(512)S(1)} %get-tuple-element.12, pred[4096]{0:T(1024)(128)(4,1)S(1)} %fusion.109), kind=kOutput, calls=%fused_computation.5 | convolution fusion | flops 279183360 | bytes 8986624 | tf_op jit(solution)/shard_map/dot_general | solution.py:36
  208.6 4.4 %multiply_convert_fusion.1 = bf16[1024,1024]{0,1:T(8,128)(2,1)} fusion(bf16[1024,64]{0,1:T(8,128)(2,1)S(1)} %copy-done.25, bf16[1024,64]{0,1:T(8,128)(2,1)S(1)} %copy-done.23, f32[1024]{0:T(1024)S(1)} %get-tuple-element.40, f32[1024]{0:T(1024)S(1)} %select_add_fusion.1, f32[1024]{0:T(1024)S(1)} %select_maximum_fusion.1, ...), kind=kOutput, calls=%fused_computation.11 | convolution fusion | flops 141557760 | bytes 6566912 | tf_op jit(solution)/shard_map/dot_general | solution.py:42
  213.0 3.1 fusion.47
  216.0 0.9 copy.99
  217.4 0.9 copy.103
  218.7 24.9 %reduce-scatter.7.cloned.1.call-done = bf16[512,64]{0,1:T(8,128)(2,1)} async-done(((bf16[4096,64]{0,1:T(8,128)(2,1)}), bf16[512,64]{0,1:T(8,128)(2,1)}) %reduce-scatter.7.cloned.1.call-update) | async-done | bytes 65552 | tf_op jit(solution)/shard_map/reduce_scatter | solution.py:182
  243.6 0.9 copy.101
  245.0 30.0 %reduce-scatter.11.cloned.1.call-done = bf16[512,64]{0,1:T(8,128)(2,1)} async-done(((bf16[4096,64]{0,1:T(8,128)(2,1)}), bf16[512,64]{0,1:T(8,128)(2,1)}) %reduce-scatter.11.cloned.1.call-update) | async-done | bytes 65552 | tf_op jit(solution)/shard_map/reduce_scatter | solution.py:185
  274.9 0.9 copy.105
  276.3 4.5 %fusion.49 = bf16[768,64]{0,1:T(8,128)(2,1)} fusion(bf16[1024,768]{1,0:T(8,128)(2,1)S(1)} %copy-done.1, bf16[1024,64]{0,1:T(8,128)(2,1)S(1)} %copy-done.25, f32[1024,64]{0,1:T(8,128)S(1)} %copy.106, f32[1024,64]{0,1:T(8,128)S(1)} %copy.104, pred[1024]{0:T(1024)(128)(4,1)S(1)} %broadcast_in_dim.304, pred[1024]{0:T(1024)(128)(4,1)S(1)} %broadcast_in_dim.295, ...), kind=kOutput, calls=%fused_computation.67 | convolution fusion | flops 240500736 | bytes 6532096 | tf_op jit(solution)/shard_map/dot_general | solution.py:36
  280.8 3.3 fusion.48
  284.8 15.0 %psum.43 = bf16[1]{0:T(256)(128)(2,1)} all-reduce(bf16[1]{0:T(256)(128)(2,1)} %bitcast.15), channel_id=1, replica_groups=mesh['slide'=2,'seq'=4,'head'=2,'rep'=2] {'seq','rep'}, use_global_device_ids=true, to_apply=%region_15.16 | all-reduce | flops 1 | bytes 4 | tf_op jit(solution)/shard_map/psum | solution.py:207
  300.5 37.9 %all-reduce.7.cloned.1.call-done = (bf16[768,64]{0,1:T(8,128)(2,1)}, bf16[768,64]{0,1:T(8,128)(2,1)}, bf16[768,64]{0,1:T(8,128)(2,1)}, bf16[64,768]{1,0:T(8,128)(2,1)}) async-done(((bf16[768,64]{0,1:T(8,128)(2,1)}, bf16[768,64]{0,1:T(8,128)(2,1)}, bf16[768,64]{0,1:T(8,128)(2,1)}, bf16[64,768]{1,0:T(8,128)(2,1)}), (bf16[768,64]{0,1:T(8,128)(2,1)}, bf16[768,64]{0,1:T(8,128)(2,1)}, bf16[768,64]{0,1:T(8,128)(2,1)}, ...) | async-done | bytes 393232 | tf_op jit(solution)/shard_map/psum | solution.py:203
  338.4 1.6 convert_element_type.176
  340.0 1.6 convert_element_type.184
  341.6 1.6 convert_element_type.195
  343.2 1.6 convert_element_type.197
  (144 shorter events, 14.6 us)
Async XLA Ops:
  7.2 97.3 %copy-start = (bf16[64,768]{1,0:T(8,128)(2,1)S(1)}, bf16[64,768]{1,0:T(8,128)(2,1)}, u32[]{:S(2)}) copy-start(bf16[64,768]{1,0:T(8,128)(2,1)} %param.17) | copy-start | bytes 294916
  7.2 24.9 %copy-start.1 = (bf16[1024,768]{1,0:T(8,128)(2,1)S(1)}, bf16[1024,768]{1,0:T(8,128)(2,1)}, u32[]{:S(2)}) copy-start(bf16[1024,768]{1,0:T(8,128)(2,1)} %param.10) | copy-start | bytes 4718596
  7.2 24.9 %copy-start.27 = (bf16[768,64]{0,1:T(8,128)(2,1)S(1)}, bf16[768,64]{0,1:T(8,128)(2,1)}, u32[]{:S(2)}) copy-start(bf16[768,64]{0,1:T(8,128)(2,1)} %param.16) | copy-start | bytes 294916
  7.2 149.3 %all-reduce.5.cloned.1.call-start = ((), (), s32[]{:S(2)}) async-start(), calls=%async_computation.4 | async-start | bytes 3145728 | tf_op jit(solution)/shard_map/psum | solution.py:121
  30.0 46.2 %copy-start.7 = (bf16[1024,64]{0,1:T(8,128)(2,1)}, bf16[1024,64]{0,1:T(8,128)(2,1)S(1)}, u32[]{:S(2)}) copy-start(bf16[1024,64]{0,1:T(8,128)(2,1)S(1)} %convolution_convert_fusion.6) | copy-start | bytes 393220
  32.1 44.1 %copy-start.9 = (bf16[1024,64]{0,1:T(8,128)(2,1)}, bf16[1024,64]{0,1:T(8,128)(2,1)S(1)}, u32[]{:S(2)}) copy-start(bf16[1024,64]{0,1:T(8,128)(2,1)S(1)} %convolution_convert_fusion.5) | copy-start | bytes 393220
  32.7 0.7 copy-start.21
  40.1 51.7 %copy-start.26 = (bf16[1024,1,64]{0,2,1:T(8,128)(2,1)}, bf16[1024,1,64]{0,2,1:T(8,128)(2,1)S(1)}, u32[]{:S(2)}) copy-start(bf16[1024,1,64]{0,2,1:T(8,128)(2,1)S(1)} %all-gather.2) | copy-start | bytes 393220
  42.4 36.6 %copy-start.11 = (bf16[1024,1,64]{0,2,1:T(8,128)(2,1)}, bf16[1024,1,64]{0,2,1:T(8,128)(2,1)S(1)}, u32[]{:S(2)}) copy-start(bf16[1024,1,64]{0,2,1:T(8,128)(2,1)S(1)} %all-gather) | copy-start | bytes 393220
  57.2 21.9 %copy-start.5 = (bf16[4096,1,64]{0,2,1:T(8,128)(2,1)}, bf16[4096,1,64]{0,2,1:T(8,128)(2,1)S(1)}, u32[]{:S(2)}) copy-start(bf16[4096,1,64]{0,2,1:T(8,128)(2,1)S(1)} %all-gather.1) | copy-start | bytes 1572868
  75.9 3.3 copy-start.18
  91.5 2.9 copy-start.24
  99.5 3.7 %copy-start.22 = (bf16[1024,64]{0,1:T(8,128)(2,1)S(1)}, bf16[1024,64]{0,1:T(8,128)(2,1)}, u32[]{:S(2)}) copy-start(bf16[1024,64]{0,1:T(8,128)(2,1)} %copy-done.21) | copy-start | bytes 393220
  99.9 3.5 copy-start.3
  104.5 60.3 %copy-start.13 = (bf16[1024,64]{0,1:T(8,128)(2,1)}, bf16[1024,64]{0,1:T(8,128)(2,1)S(1)}, u32[]{:S(2)}) copy-start(bf16[1024,64]{0,1:T(8,128)(2,1)S(1)} %fusion.58) | copy-start | bytes 393220
  106.3 109.7 %reduce-scatter.5.cloned.1.call-start = ((), (), s32[]{:S(2)}) async-start(), calls=%async_computation.5 | async-start | bytes 196608 | tf_op jit(solution)/shard_map/reduce_scatter | solution.py:174
  107.3 52.0 %copy-start.30 = (f32[768]{0:T(1024)S(1)}, f32[768]{0:T(1024)}, u32[]{:S(2)}) copy-start(f32[768]{0:T(1024)} %param.18) | copy-start | bytes 9220
  107.3 52.0 %copy-start.33 = (bf16[768,8]{0,1:T(8,128)(2,1)S(1)}, bf16[768,8]{0,1:T(8,128)(2,1)}, u32[]{:S(2)}) copy-start(bf16[768,8]{0,1:T(8,128)(2,1)} %param.19) | copy-start | bytes 36868
  156.5 2.0 copy-start.4
  159.3 0.9 copy-start.31
  170.7 2.9 copy-start.29
  173.6 2.5 copy-start.12
  173.6 3.6 %copy-start.20 = (bf16[512,1,64]{0,2,1:T(8,128)(2,1)S(1)}, bf16[512,1,64]{0,2,1:T(8,128)(2,1)}, u32[]{:S(2)}) copy-start(bf16[512,1,64]{0,2,1:T(8,128)(2,1)} %copy.78) | copy-start | bytes 196612
  173.6 4.6 %copy-start.17 = (bf16[512,1,64]{2,1,0:T(2,128)(2,1)S(1)}, bf16[512,1,64]{2,1,0:T(2,128)(2,1)}, u32[]{:S(2)}) copy-start(bf16[512,1,64]{2,1,0:T(2,128)(2,1)} %get-tuple-element.22) | copy-start | bytes 196612
  176.2 7.1 %copy-start.32 = (f32[512]{0:T(512)S(1)}, f32[512]{0:T(512)}, u32[]{:S(2)}) copy-start(f32[512]{0:T(512)} %get-tuple-element.10) | copy-start | bytes 6148
  179.0 38.4 %reduce-scatter.9.cloned.1.call-start = ((), (), s32[]{:S(2)}) async-start(), calls=%async_computation.7 | async-start | bytes 196608 | tf_op jit(solution)/shard_map/reduce_scatter | solution.py:177
  183.3 8.3 %copy-start.6 = (bf16[4096,1,64]{0,2,1:T(8,128)(2,1)S(1)}, bf16[4096,1,64]{0,2,1:T(8,128)(2,1)}, u32[]{:S(2)}) copy-start(bf16[4096,1,64]{0,2,1:T(8,128)(2,1)} %copy-done.5) | copy-start | bytes 1572868
  189.6 2.0 copy-start.2
  191.6 6.1 %copy-start.19 = (bf16[512,1,64]{0,2,1:T(8,128)(2,1)S(1)}, bf16[512,1,64]{0,2,1:T(8,128)(2,1)}, u32[]{:S(2)}) copy-start(bf16[512,1,64]{0,2,1:T(8,128)(2,1)} %copy.81) | copy-start | bytes 196612
  193.9 7.8 %copy-start.14 = (bf16[1024,64]{0,1:T(8,128)(2,1)S(1)}, bf16[1024,64]{0,1:T(8,128)(2,1)}, u32[]{:S(2)}) copy-start(bf16[1024,64]{0,1:T(8,128)(2,1)} %copy-done.13) | copy-start | bytes 393220
  197.7 5.1 %copy-start.28 = (bf16[512,1,64]{0,2,1:T(8,128)(2,1)S(1)}, bf16[512,1,64]{0,2,1:T(8,128)(2,1)}, u32[]{:S(2)}) copy-start(bf16[512,1,64]{0,2,1:T(8,128)(2,1)} %copy.96) | copy-start | bytes 196612
  201.6 42.0 %reduce-scatter.7.cloned.1.call-start = ((), (), s32[]{:S(2)}) async-start(), calls=%async_computation.6 | async-start | bytes 589824 | tf_op jit(solution)/shard_map/reduce_scatter | solution.py:182
  202.7 5.8 %copy-start.23 = (bf16[1024,64]{0,1:T(8,128)(2,1)S(1)}, bf16[1024,64]{0,1:T(8,128)(2,1)}, u32[]{:S(2)}) copy-start(bf16[1024,64]{0,1:T(8,128)(2,1)} %copy-done.21) | copy-start | bytes 393220
  202.8 5.8 %copy-start.25 = (bf16[1024,64]{0,1:T(8,128)(2,1)S(1)}, bf16[1024,64]{0,1:T(8,128)(2,1)}, u32[]{:S(2)}) copy-start(bf16[1024,64]{0,1:T(8,128)(2,1)} %get-tuple-element.41) | copy-start | bytes 393220
  202.8 72.2 %reduce-scatter.11.cloned.1.call-start = ((), (), s32[]{:S(2)}) async-start(), calls=%async_computation.8 | async-start | bytes 589824 | tf_op jit(solution)/shard_map/reduce_scatter | solution.py:185
  208.5 4.5 %copy-start.10 = (bf16[1024,64]{0,1:T(8,128)(2,1)S(1)}, bf16[1024,64]{0,1:T(8,128)(2,1)}, u32[]{:S(2)}) copy-start(bf16[1024,64]{0,1:T(8,128)(2,1)} %copy-done.9) | copy-start | bytes 393220
  208.5 4.5 %copy-start.15 = (f32[1024,64]{0,1:T(8,128)S(1)}, f32[1024,64]{0,1:T(8,128)}, u32[]{:S(2)}) copy-start(f32[1024,64]{0,1:T(8,128)} %copy.95) | copy-start | bytes 786436
  208.5 4.5 %copy-start.16 = (f32[1024,64]{0,1:T(8,128)S(1)}, f32[1024,64]{0,1:T(8,128)}, u32[]{:S(2)}) copy-start(f32[1024,64]{0,1:T(8,128)} %copy.98) | copy-start | bytes 786436
  208.5 130.0 %all-reduce.7.cloned.1.call-start = ((), (), s32[]{:S(2)}) async-start(), calls=%async_computation.9 | async-start | bytes 786432 | tf_op jit(solution)/shard_map/psum | solution.py:203
  276.3 4.5 %copy-start.8 = (bf16[1024,64]{0,1:T(8,128)(2,1)S(1)}, bf16[1024,64]{0,1:T(8,128)(2,1)}, u32[]{:S(2)}) copy-start(bf16[1024,64]{0,1:T(8,128)(2,1)} %copy-done.7) | copy-start | bytes 393220
Sparse Core Ops, SparseCore 0:
  106.4 50.0 all-reduce.4
  179.1 7.5 reduce-scatter.4
  201.8 7.5 reduce-scatter.8
  211.5 32.0 reduce-scatter.6
  245.7 29.1 reduce-scatter.10
  284.3 54.1 all-reduce.6
where the time goes:
time: 359 us; the launch traced here: 353 us
  waiting for transfers between devices  142 us (40%)
  matrix products  70.3 us (20%)
  blocking collectives  60.3 us (17%)
  local copies, waits for them, and re-layouts  32.9 us (9%)
  other arithmetic  24.5 us (7%)
  between operations  22.4 us (6%)
    psum x1, waiting for transfers between devices, body(): lax.psum(partial_mix.astype(jnp.bfloat16), 'head').astype(jnp.float32)  49.1 us
    psum x1, waiting for transfers between devices, body(): lax.psum(grad_query.astype(jnp.bfloat16), ('seq', 'rep'))  37.9 us
    reduce_scatter x1, waiting for transfers between devices, body(): lax.psum_scatter(key_terms[2][1].astype(jnp.bfloat16), ('seq', 'rep'), sc...  30 us
    dot_general x8, matrix products, contract_rows(): lax.dot_general(left, right, (((0,), (0,)), ((), ())), preferred_element_...  25.3 us
    reduce_scatter x1, waiting for transfers between devices, body(): lax.psum_scatter(key_terms[2][0].astype(jnp.bfloat16), ('seq', 'rep'), sc...  24.9 us
    all_gather x1, blocking collectives, body(): lax.all_gather(select(values, distant_offset, far_stride), ('seq', 'rep')...  16 us
    psum x1, blocking collectives, body(): lax.psum(loss_part.reshape(1).astype(jnp.bfloat16), ('seq', 'rep'))  15 us
    all_gather x1, blocking collectives, body(): lax.all_gather(select(keys, distant_offset, far_stride), ('seq', 'rep'),...  14.8 us
  transfers between devices with their start and end apart: 6, of which 4 were waited for; matrix products, arithmetic and copies ran while one was open for 11% of the time, Pallas kernels for 0%

commit v1 on v0

v1 whole, which is shorter than its diff:
```python
import functools
import math

import jax
import jax.numpy as jnp
from jax import lax
from jax.experimental import pallas as pl
from jax.experimental.pallas import tpu as pltpu
from jax.sharding import PartitionSpec as P

MESH = pl.DeviceIdType.MESH
F32, BF16 = jnp.float32, jnp.bfloat16
LOW = -1e30
PERM = 256
TAIL = 16


def nn(a, b):
    return jnp.dot(a, b, preferred_element_type=F32)


def nt(a, b):
    return lax.dot_general(a, b, (((1,), (1,)), ((), ())), preferred_element_type=F32)


def tn(a, b):
    return lax.dot_general(a, b, (((0,), (0,)), ((), ())), preferred_element_type=F32)


def lanes(rows):
    return lax.broadcasted_iota(jnp.int32, (rows, 128), 1)


def subs(rows):
    return lax.broadcasted_iota(jnp.int32, (rows, 128), 0)


def three(x):
    hi = x.astype(BF16).astype(F32)
    rest = x - hi
    mid = rest.astype(BF16).astype(F32)
    return hi, mid, rest - mid


def kernel(
    dims,
    tiles, labels, counts, offsets, wqkv, w_out, gain, wcc,
    res, loss_out,
    xt, qs, kvs, ka0, va0, kv_all, ka2, va2, pr, ka1, va1, att_pk, wo,
    acc0, m0, acc1, m1, qa, doa, atb, dmix, dq, dqp, dkv, dkvp,
    rs_out, rs_sib, rs_mid, rs_z, pr_out, pr_in, lt, ltz,
    pan, pan_sib, pan_half, pan_z,
    s_far, r_far, s_fwd, r_fwd, s_pr, r_pr, s_w, r_w, s_att, r_att,
    s_rs, r_rs, s_rz, r_rz, s_pb, r_pb, s_l, r_l, s_lz, r_lz,
    s_a1, r_a1, s_a2, r_a2, s_a3, r_a3, s_a4, r_a4,
):
    ns, nh, ps, fs, hs, classes, piece = dims
    n, d = tiles.shape
    far, half = n // fs, n // ps
    sub_count = fs // ps
    z, h, p = lax.axis_index("seq"), lax.axis_index("head"), lax.axis_index("rep")

    def at_z(dz):
        return {"seq": lax.rem(z + dz, ns)}

    def at_p(dp):
        return {"rep": lax.rem(p + dp, ps)}

    def at_h(dh):
        return {"head": lax.rem(h + dh, nh)}

    sends = []

    def push(src, dst, ssem, rsem, where):
        copy = pltpu.make_async_remote_copy(
            src_ref=src, dst_ref=dst, send_sem=ssem, recv_sem=rsem,
            device_id=where, device_id_type=MESH,
        )
        copy.start()
        sends.append(copy)
        return copy

    barrier = pltpu.get_barrier_semaphore()
    peers = (
        [at_z(i) for i in range(1, ns)]
        + [at_p(i) for i in range(1, ps)]
        + [at_h(i) for i in range(1, nh)]
    )
    for peer in peers:
        pl.semaphore_signal(barrier, inc=1, device_id=peer, device_id_type=MESH)

    residues = [(c % sub_count) * ps + c // sub_count for c in range(fs)]
    count = counts[0]
    o1 = offsets[0, 0]
    o2 = offsets[1, 0]
    c2 = lax.rem(o2, ps) * sub_count + lax.div(o2, ps)

    def rows_of(c):
        return pl.ds(c * far, far)

    per = PERM // fs
    a = lax.broadcasted_iota(jnp.int32, (PERM, PERM), 0)
    b = lax.broadcasted_iota(jnp.int32, (PERM, PERM), 1)
    want = jnp.zeros((PERM, PERM), jnp.int32)
    for c in range(fs):
        want = jnp.where((a >= c * per) & (a < (c + 1) * per), (a - c * per) * fs + residues[c], want)
    perm = (want == b).astype(F32).astype(BF16)
    for blk in range(n // PERM):
        moved = nn(perm, tiles[pl.ds(blk * PERM, PERM), :]).astype(BF16)
        qkv = nn(moved, wqkv[...])
        q_part = (qkv[:, :128] * (1.0 / math.sqrt(hs))).astype(BF16)
        kv_part = qkv[:, 128:].astype(BF16)
        for c in range(fs):
            spot = pl.ds(c * far + blk * per, per)
            xt[spot, :] = moved[c * per:(c + 1) * per, :]
            qs[spot, :] = q_part[c * per:(c + 1) * per, :]
            kvs[spot, :] = kv_part[c * per:(c + 1) * per, :]

    def pick_far(ref):
        out = ref[rows_of(0), :].astype(F32)
        for c in range(1, fs):
            out = jnp.where(c2 == c, ref[rows_of(c), :].astype(F32), out)
        return out

    def pick_half(ref):
        out = ref[pl.ds(0, half), :].astype(F32)
        for c in range(1, ps):
            out = jnp.where(o1 == c, ref[pl.ds(c * half, half), :].astype(F32), out)
        return out

    high = lax.div(count, 256)
    tail = jnp.where(subs(TAIL) < 8, high.astype(F32), (count - high * 256).astype(F32)).astype(BF16)
    kv_all[0, 0, pl.ds(0, far), :] = pick_far(kvs).astype(BF16)
    kv_all[0, 0, pl.ds(far, TAIL), :] = tail
    pr[0, pl.ds(0, half), :] = pick_half(kvs).astype(BF16)
    pr[0, pl.ds(half, TAIL), :] = tail

    wo[:, pl.ds(0, hs), :] = jnp.zeros((nh, hs, d), BF16)
    wo[:, pl.ds(2 * hs, hs), :] = jnp.zeros((nh, hs, d), BF16)
    wo[0, pl.ds(hs, hs), :] = w_out[...]

    pl.semaphore_wait(barrier, len(peers))
    far_z = {}
    for dz in range(1, ns):
        far_z[dz] = push(kv_all.at[0, 0], kv_all.at[dz, 0], s_far.at[dz], r_far.at[dz], at_z(dz))
    pr_c, fwd_c, w_c, att_c = {}, {}, {}, {}
    for dp in range(1, ps):
        pr_c[dp] = push(pr.at[0], pr.at[dp], s_pr.at[dp], r_pr.at[dp], at_p(dp))
        fwd_c[0, dp] = push(kv_all.at[0, 0], kv_all.at[0, dp], s_fwd.at[0, dp], r_fwd.at[0, dp], at_p(dp))
    for dh in range(1, nh):
        w_c[dh] = push(
            wo.at[0, pl.ds(hs, hs), :], wo.at[dh, pl.ds(hs, hs), :], s_w.at[dh], r_w.at[dh], at_h(dh)
        )

    def augment(kv, original, cnt):
        rows = kv.shape[0]
        lane = lanes(rows)
        kv = kv.astype(F32)
        bias = jnp.where(original.astype(F32) < cnt, 0.0, LOW)
        key = jnp.where(lane < hs, kv, jnp.where(lane == hs, bias, 1.0))
        value = jnp.where(lane < hs, 1.0, kv)
        return key.astype(BF16), value.astype(BF16)

    def remote_count(tail):
        tail = tail.astype(F32)
        return tail[0:1, 0:1] * 256.0 + tail[8:9, 0:1]

    def with_one(q):
        return jnp.where(lanes(q.shape[0]) == hs, 1.0, q.astype(F32)).astype(BF16)

    def forward(q, key, value):
        s = nt(q, key)
        top = jnp.max(s, axis=-1, keepdims=True)
        return top, nn(jnp.exp(s - top).astype(BF16), value)

    own_count = count.astype(F32)
    step = min(256, far)
    for c in range(fs):
        key, value = augment(kvs[rows_of(c), :], subs(far) * fs + residues[c], own_count)
        ka0[rows_of(c), :] = key
        va0[rows_of(c), :] = value
    wide = min(256, n)
    for i in range(n // wide):
        spot = pl.ds(i * wide, wide)
        top, acc = forward(with_one(qs[spot, :]), ka0[...], va0[...])
        m0[spot, :] = jnp.broadcast_to(top, (wide, 128))
        acc0[spot, :] = acc
    for dp in range(ps):
        if dp:
            pr_c[dp].wait_recv()
        cnt = remote_count(pr[dp, pl.ds(half, TAIL), :])
        for k in range(sub_count):
            key, value = augment(pr[dp, pl.ds(k * far, far), :], subs(far) * fs + k * ps + o1, cnt)
            ka1[pl.ds(dp * half + k * far, far), :] = key
            va1[pl.ds(dp * half + k * far, far), :] = value
    q_half = with_one(pick_half(qs))
    wide = min(256, half)
    for i in range(half // wide):
        spot = pl.ds(i * wide, wide)
        top, acc = forward(q_half[i * wide:(i + 1) * wide, :], ka1[...], va1[...])
        m1[spot, :] = jnp.broadcast_to(top, (wide, 128))
        acc1[spot, :] = acc

    q_far = with_one(pick_far(qs))
    order = [(0, dp) for dp in range(ps)]
    for dz in range(1, ns):
        order += [(dz, dp) for dp in range(ps)]
    top2 = acc2 = None
    for dz in range(1, ns):
        far_z[dz].wait_recv()
        for dp in range(1, ps):
            fwd_c[dz, dp] = push(
                kv_all.at[dz, 0], kv_all.at[dz, dp], s_fwd.at[dz, dp], r_fwd.at[dz, dp], at_p(dp)
            )
        for bz, dp in [(dz - 1, i) for i in range(ps)] + ([(dz, i) for i in range(ps)] if dz == ns - 1 else []):
            if dp:
                fwd_c[bz, dp].wait_recv()
            key, value = augment(
                kv_all[bz, dp, pl.ds(0, far), :], subs(far) * fs + o2,
                remote_count(kv_all[bz, dp, pl.ds(far, TAIL), :]),
            )
            ka2[bz * ps + dp] = key
            va2[bz * ps + dp] = value
            top, acc = forward(q_far, key, value)
            if top2 is None:
                top2, acc2 = top, acc
            else:
                both = jnp.maximum(top, top2)
                acc2 = acc2 * jnp.exp(top2 - both) + acc * jnp.exp(top - both)
                top2 = both

    for c in range(fs):
        rows = rows_of(c)
        in_half = pl.ds((c % sub_count) * far, far)
        t0 = m0[rows, 0:1]
        t1 = jnp.where(o1 == c // sub_count, m1[in_half, 0:1], LOW)
        t2 = jnp.where(c2 == c, top2, LOW)
        top = jnp.maximum(t0, jnp.maximum(t1, t2))
        acc = acc0[rows, :] * jnp.exp(t0 - top) + acc1[in_half, :] * jnp.exp(t1 - top) + acc2 * jnp.exp(t2 - top)
        total = acc[:, 0:1]
        lane = lanes(far)
        att = jnp.where(lane < hs, 0.0, acc / total)
        atb[rows, :] = att.astype(BF16)
        one, two, rest = three(-(top + jnp.log(total)))
        aux = jnp.where(lane == hs, 1.0, jnp.where(lane == hs + 1, one, jnp.where(lane == hs + 2, two, jnp.where(lane == hs + 3, rest, 0.0))))
        qa[rows, :] = jnp.where(lane < hs, qs[rows, :].astype(F32), aux).astype(BF16)
    mid = n // 2
    att_pk[0, :, :] = (
        atb[pl.ds(0, mid), :].astype(F32) + pltpu.roll(atb[pl.ds(mid, mid), :].astype(F32), hs, 1)
    ).astype(BF16)
    for dh in range(1, nh):
        att_c[dh] = push(att_pk.at[0], att_pk.at[dh], s_att.at[dh], r_att.at[dh], at_h(dh))
    for dh in range(1, nh):
        w_c[dh].wait_recv()
    for dh in range(1, nh):
        att_c[dh].wait_recv()

    loss = jnp.zeros((1, 1), F32)
    g = gain[...]
    for i in range(n // step):
        start = i * step
        c, inner = start // far, start % far
        rows = pl.ds(start, step)
        mixed = xt[rows, :].astype(F32)
        for dh in range(nh):
            if start < mid:
                term = nn(att_pk[dh, pl.ds(start, step), :], wo[dh, pl.ds(0, 2 * hs), :])
            else:
                term = nn(att_pk[dh, pl.ds(start - mid, step), :], wo[dh, pl.ds(hs, 2 * hs), :])
            mixed = mixed + term.astype(BF16).astype(F32)
        center = mixed - jnp.mean(mixed, axis=-1, keepdims=True)
        inv_dev = lax.rsqrt(jnp.mean(center * center, axis=-1, keepdims=True) + 1e-05)
        normal = center * inv_dev
        normed = (normal * g).astype(BF16)
        logits = nt(wcc[...], normed)[:classes, :]
        peak = jnp.max(logits, axis=0, keepdims=True)
        log_total = jnp.log(jnp.sum(jnp.exp(logits - peak), axis=0, keepdims=True)) + peak
        kind = lax.broadcasted_iota(jnp.int32, (classes, step), 0)
        onehot = (kind == labels[:, pl.ds(start, step)]).astype(F32)
        spot = lax.broadcasted_iota(jnp.int32, (1, step), 1)
        ok = ((spot + inner) * fs + residues[c] < count).astype(F32)
        cross = log_total - jnp.sum(onehot * logits, axis=0, keepdims=True)
        loss = loss + jnp.sum(ok * cross, axis=1, keepdims=True)
        d_logits = (jnp.exp(logits - log_total) - onehot) * ok * (1.0 / n)
        hi = d_logits.astype(BF16).astype(F32)
        split = jnp.concatenate([hi, d_logits - hi], axis=0).astype(BF16)
        d_normal = tn(split, wcc[...]) * g
        d_mixed = inv_dev * (
            d_normal
            - jnp.mean(d_normal, axis=-1, keepdims=True)
            - normal * jnp.mean(d_normal * normal, axis=-1, keepdims=True)
        )
        d_mixed = d_mixed.astype(BF16)
        dmix[rows, :] = d_mixed
        d_att = nt(d_mixed, wo[0, pl.ds(0, 2 * hs), :]).astype(BF16).astype(F32)
        delta = jnp.sum(d_att * atb[rows, :].astype(F32), axis=-1, keepdims=True)
        one, two, rest = three(-delta)
        lane = lanes(step)
        aux = jnp.where(lane == 0, one, jnp.where(lane == 1, two, jnp.where(lane == 2, rest, d_att)))
        doa[rows, :] = aux.astype(BF16)
    lt[0, :, :] = jnp.broadcast_to(loss * (1.0 / n), (8, 128))
    lt_c = {dp: push(lt.at[0], lt.at[dp], s_l.at[dp], r_l.at[dp], at_p(dp)) for dp in range(1, ps)}

    def backward(q, do, key, value):
        prob = jnp.exp(nt(key, q))
        d_score = (prob * nt(value, do)).astype(BF16)
        d_key = nn(d_score, q)
        d_value = nn(prob.astype(BF16), do)
        return tn(d_score, key), jnp.where(lanes(key.shape[0]) < hs, d_key, d_value)

    q_far = pick_far(qa).astype(BF16)
    do_far = pick_far(doa).astype(BF16)
    dq_far = None
    rz_c = {}
    own_far = None
    for dz in list(range(1, ns)) + [0]:
        rs_c = {}
        own = None
        for dp in list(range(1, ps)) + [0]:
            key_rows = dz * ps + dp
            d_q, d_kv = backward(q_far, do_far, ka2[key_rows], va2[key_rows])
            dq_far = d_q if dq_far is None else dq_far + d_q
            if dp:
                rs_out[dz, dp] = d_kv.astype(BF16)
                rs_c[dp] = push(
                    rs_out.at[dz, dp], rs_sib.at[dz, dp], s_rs.at[dz, dp], r_rs.at[dz, dp], at_p(ps - dp)
                )
            else:
                own = d_kv
        for dp in range(1, ps):
            rs_c[dp].wait_recv()
            own = own + rs_sib[dz, dp].astype(F32)
        if dz:
            rs_mid[dz] = own.astype(BF16)
            rz_c[dz] = push(rs_mid.at[dz], rs_z.at[dz], s_rz.at[dz], r_rz.at[dz], at_z(ns - dz))
        else:
            own_far = own

    whole_loss = lt[0, :, :]
    for dp in range(1, ps):
        lt_c[dp].wait_recv()
        whole_loss = whole_loss + lt[dp, :, :]
    ltz[0, :, :] = whole_loss
    lz_c = {dz: push(ltz.at[0], ltz.at[dz], s_lz.at[dz], r_lz.at[dz], at_z(dz)) for dz in range(1, ns)}

    q_half = pick_half(qa).astype(BF16)
    do_half = pick_half(doa).astype(BF16)
    pb_c = {}
    dq_half = None
    for dp in list(range(1, ps)) + [0]:
        key_rows = pl.ds(dp * half, half)
        d_q, d_kv = backward(q_half, do_half, ka1[key_rows, :], va1[key_rows, :])
        dq_half = d_q if dq_half is None else dq_half + d_q
        if dp:
            pr_out[dp] = d_kv.astype(BF16)
            pb_c[dp] = push(pr_out.at[dp], pr_in.at[dp], s_pb.at[dp], r_pb.at[dp], at_p(ps - dp))
        else:
            dkvp[...] = d_kv
    dqp[...] = dq_half

    tile = min(512, n)
    for j in range(n // tile):
        key_rows = pl.ds(j * tile, tile)
        total = None
        for i in range(n // tile):
            rows = pl.ds(i * tile, tile)
            d_q, d_kv = backward(qa[rows, :], doa[rows, :], ka0[key_rows, :], va0[key_rows, :])
            total = d_kv if total is None else total + d_kv
            if j:
                dq[rows, :] += d_q
            else:
                dq[rows, :] = d_q
        dkv[key_rows, :] = total

    for c in range(fs):
        rows = rows_of(c)
        in_half = pl.ds((c % sub_count) * far, far)
        part = dq[rows, :]
        part = part + jnp.where(o1 == c // sub_count, dqp[in_half, :], 0.0)
        part = part + jnp.where(c2 == c, dq_far, 0.0)
        qa[rows, :] = jnp.where(lanes(far) < hs, part * (1.0 / math.sqrt(hs)), 0.0).astype(BF16)

    quarter = ns * piece
    first, second, third, fourth = {}, {}, {}, {}

    def start_panel(k, panel):
        pan[k, pl.ds(0, d), :] = panel.astype(BF16)
        if quarter * ps > d:
            pan[k, pl.ds(d, quarter * ps - d), :] = jnp.zeros((quarter * ps - d, 128), BF16)
        for dp in range(1, ps):
            there = pl.multiple_of(lax.rem(p + dp, ps) * quarter, 16)
            first[k, dp] = push(
                pan.at[k, pl.ds(there, quarter), :], pan_sib.at[k, dp],
                s_a1.at[k, dp], r_a1.at[k, dp], at_p(dp),
            )

    def second_panel(k):
        here = pl.multiple_of(p * quarter, 16)
        total = pan[k, pl.ds(here, quarter), :].astype(F32)
        for dp in range(1, ps):
            first[k, dp].wait_recv()
            total = total + pan_sib[k, dp].astype(F32)
        pan_half[k] = total.astype(BF16)
        for dz in range(1, ns):
            there = pl.multiple_of(lax.rem(z + dz, ns) * piece, 16)
            second[k, dz] = push(
                pan_half.at[k, pl.ds(there, piece), :], pan_z.at[k, dz],
                s_a2.at[k, dz], r_a2.at[k, dz], at_z(dz),
            )

    def third_panel(k):
        here = pl.multiple_of(z * piece, 16)
        total = pan_half[k, pl.ds(here, piece), :].astype(F32)
        for dz in range(1, ns):
            second[k, dz].wait_recv()
            total = total + pan_z[k, dz].astype(F32)
        spot = pl.ds(pl.multiple_of(p * quarter + z * piece, 16), piece)
        res[k, spot, :] = total.astype(BF16)
        for dz in range(1, ns):
            third[k, dz] = push(
                res.at[k, spot, :], res.at[k, spot, :], s_a3.at[k, dz], r_a3.at[k, dz], at_z(dz)
            )

    def fourth_panel(k):
        for dz in range(1, ns):
            third[k, dz].wait_recv()
        spot = pl.ds(pl.multiple_of(p * quarter, 16), quarter)
        for dp in range(1, ps):
            fourth[k, dp] = push(
                res.at[k, spot, :], res.at[k, spot, :], s_a4.at[k, dp], r_a4.at[k, dp], at_p(dp)
            )

    start_panel(0, tn(xt[...], qa[...]) + tn(dmix[...], atb[...]))

    half_sum = dkvp[...]
    for dp in range(1, ps):
        pb_c[dp].wait_recv()
        half_sum = half_sum + pr_in[dp].astype(F32)
    dkvp[...] = half_sum
    for dz in range(1, ns):
        rz_c[dz].wait_recv()
        own_far = own_far + rs_z[dz].astype(F32)
    for c in range(fs):
        rows = rows_of(c)
        in_half = pl.ds((c % sub_count) * far, far)
        part = dkv[rows, :]
        part = part + jnp.where(o1 == c // sub_count, dkvp[in_half, :], 0.0)
        part = part + jnp.where(c2 == c, own_far, 0.0)
        doa[rows, :] = part.astype(BF16)
    second_panel(0)
    start_panel(1, tn(xt[...], doa[...]))
    third_panel(0)
    second_panel(1)
    fourth_panel(0)
    third_panel(1)
    total = ltz[0, :, :]
    for dz in range(1, ns):
        lz_c[dz].wait_recv()
        total = total + ltz[dz, :, :]
    loss_out[...] = total
    fourth_panel(1)
    for k in range(2):
        for dp in range(1, ps):
            fourth[k, dp].wait_recv()
    for copy in sends:
        copy.wait_send()


def body(ns, nh, ps, tiles, labels, counts, offsets, w_query, w_key, w_value, w_out, ln_gain, w_class):
    n, d = tiles.shape
    hs = w_query.shape[1]
    classes = w_class.shape[1]
    shards = ns * ps
    fs = shards // 4
    far, half = n // fs, n // ps
    piece = -(-d // (shards * 16)) * 16
    quarter = ns * piece
    labels_row = labels.reshape(far, fs // ps, ps).transpose(2, 1, 0).reshape(1, n)
    wqkv = jnp.concatenate([w_query, jnp.zeros((d, 128 - hs), BF16), w_key, w_value], axis=1)
    wcc = jnp.concatenate([w_class.T, w_class.T], axis=0)
    vmem = pltpu.VMEM
    dma = lambda *shape: pltpu.SemaphoreType.DMA(shape)
    scratch = [
        vmem((n, d), BF16), vmem((n, 128), BF16), vmem((n, 128), BF16),
        vmem((n, 128), BF16), vmem((n, 128), BF16),
        vmem((ns, ps, far + TAIL, 128), BF16),
        vmem((shards, far, 128), BF16), vmem((shards, far, 128), BF16),
        vmem((ps, half + TAIL, 128), BF16), vmem((n, 128), BF16), vmem((n, 128), BF16),
        vmem((nh, n // 2, 128), BF16), vmem((nh, 3 * hs, d), BF16),
        vmem((n, 128), F32), vmem((n, 128), F32), vmem((half, 128), F32), vmem((half, 128), F32),
        vmem((n, 128), BF16), vmem((n, 128), BF16), vmem((n, 128), BF16), vmem((n, d), BF16),
        vmem((n, 128), F32), vmem((half, 128), F32), vmem((n, 128), F32), vmem((half, 128), F32),
        vmem((ns, ps, far, 128), BF16), vmem((ns, ps, far, 128), BF16),
        vmem((ns, far, 128), BF16), vmem((ns, far, 128), BF16),
        vmem((ps, half, 128), BF16), vmem((ps, half, 128), BF16),
        vmem((ps, 8, 128), F32), vmem((ns, 8, 128), F32),
        vmem((2, ps * quarter, 128), BF16), vmem((2, ps, quarter, 128), BF16),
        vmem((2, quarter, 128), BF16), vmem((2, ns, piece, 128), BF16),
        dma(ns), dma(ns), dma(ns, ps), dma(ns, ps), dma(ps), dma(ps), dma(nh), dma(nh), dma(nh), dma(nh),
        dma(ns, ps), dma(ns, ps), dma(ns), dma(ns), dma(ps), dma(ps), dma(ps), dma(ps), dma(ns), dma(ns),
        dma(2, ps), dma(2, ps), dma(2, ns), dma(2, ns), dma(2, ns), dma(2, ns), dma(2, ps), dma(2, ps),
    ]
    whole = pl.BlockSpec(memory_space=pltpu.VMEM)
    scalar = pl.BlockSpec(memory_space=pltpu.SMEM)
    res, loss = pl.pallas_call(
        functools.partial(kernel, (ns, nh, ps, fs, hs, classes, piece)),
        out_shape=(
            jax.ShapeDtypeStruct((2, ps * quarter, 128), BF16),
            jax.ShapeDtypeStruct((8, 128), F32),
        ),
        in_specs=[whole, whole, scalar, scalar, whole, whole, whole, whole],
        out_specs=(whole, whole),
        scratch_shapes=scratch,
        compiler_params=pltpu.CompilerParams(
            collective_id=0, has_side_effects=True, vmem_limit_bytes=56 * 1024 * 1024
        ),
    )(tiles, labels_row, counts, offsets, wqkv, w_out, ln_gain.reshape(1, d), wcc)
    wide = res[:, :d, :].astype(F32)
    return (
        loss[0, :1], wide[0, :, :hs], wide[1, :, :hs], wide[1, :, hs:], wide[0, :, hs:].T,
    )


def solution(mesh):
    placed = (
        P(("slide", "seq", "rep"), None),
        P(("slide", "seq", "rep")),
        P(("slide", "seq", "rep")),
        P(None, "head"),
        P(None, "head"),
        P(None, "head"),
        P(None, "head"),
        P("head", None),
        P(),
        P(),
    )
    sizes = mesh.shape
    return jax.shard_map(
        functools.partial(body, sizes["seq"], sizes["head"], sizes["rep"]),
        mesh=mesh,
        in_specs=placed,
        out_specs=(
            P("slide"),
            P("slide", "head"),
            P("slide", "head"),
            P("slide", "head"),
            P("head", "slide"),
        ),
        check_vma=False,
    )
```

time: 359 us -> 83.9 us (0.23); the launches traced: 353 us -> 83.5 us
  waiting for transfers between devices: 142 us -> 0 us
  matrix products: 70.3 us -> 0 us
  Pallas kernels: 0 us -> 67.3 us
  blocking collectives: 60.3 us -> 0 us
  local copies, waits for them, and re-layouts: 32.9 us -> 11.5 us
  other arithmetic: 24.5 us -> 3.36 us
  between operations: 22.4 us -> 1.34 us
    psum x2 -> x0, waiting for transfers between devices: 87.1 us -> none  [the longest x1 49.1 us: body(): lax.psum(partial_mix.astype(jnp.bfloat16), 'head').astype(jnp.float32)]
    dot_general x26 -> x0, matrix products: 70.3 us -> none  [the longest x8 25.3 us: contract_rows(): lax.dot_general(left, right, (((0,), (0,)), ((), ())), preferred_element_...]
    pallas_call x0 -> x1, Pallas kernels: none -> 67.3 us  [body(): pl.pallas_call(functools.partial(kernel, (ns, nh, ps, fs, hs, classes, pi...]
    reduce_scatter x4 -> x0, waiting for transfers between devices: 55 us -> none  [the longest x1 30 us: body(): lax.psum_scatter(key_terms[2][1].astype(jnp.bfloat16), ('seq', 'rep'), sc...]
    all_gather x4 -> x0, blocking collectives: 34.6 us -> none  [the longest x1 16 us: body(): lax.all_gather(select(values, distant_offset, far_stride), ('seq', 'rep')...]
    psum x1 -> x0, blocking collectives: 15 us -> none  [body(): lax.psum(loss_part.reshape(1).astype(jnp.bfloat16), ('seq', 'rep'))]
    reduce_sum x9 -> x0, other arithmetic: 13.7 us -> none  [the longest x3 9.89 us: body(): jnp.sum(expo, axis=-1)]
    unnamed x1 -> x0, blocking collectives: 10.6 us -> none
  transfers between devices with their start and end apart: 6 -> 0, of which waited for: 4 -> 0; matrix products, arithmetic and copies ran while one was open for 11% -> 0% of each run, Pallas kernels for 0% -> 0%
where the time goes in v1:
time: 83.9 us; the launch traced here: 83.5 us
  Pallas kernels  67.3 us (80%)
  local copies, waits for them, and re-layouts  11.5 us (14%)
  other arithmetic  3.36 us (4%)
  between operations  1.34 us (2%)
    pallas_call x1, Pallas kernels, body(): pl.pallas_call(functools.partial(kernel, (ns, nh, ps, fs, hs, classes, pi...  67.3 us
    unnamed x11, local copies, waits for them, and re-layouts  8.4 us

profile of v1, /device:TPU:0, one launch (start us, length us, event | category | flops | bytes accessed | tf_op | source)
XLA Modules:
  0.0 83.5 jit_solution(11096608363065175514)
XLA Ops:
  0.6 0.0 copy-start
  1.3 0.1 pad.3.clone
  1.4 1.3 %copy.27.offsets = s32[2,1]{1,0:T(2,128)} copy(s32[2,1]{0,1:T(1,128)} %param.13) | data formatting | bytes 16 | tf_op args[3]
  2.7 1.3 %reshape.21.gain = f32[1,768]{1,0:T(1,128)} reshape(f32[768]{0:T(1024)} %param.18) | data formatting | bytes 6144 | tf_op jit(solution)/shard_map/reshape | solution.py:517
  4.0 1.4 %pad_maximum_fusion.1.wcc = bf16[16,768]{1,0:T(8,128)(2,1)} fusion(bf16[8,768]{1,0:T(8,128)(2,1)} %bitcast.19), kind=kLoop, calls=%fused_computation.5 | loop fusion | flops 49152 | bytes 36864 | tf_op jit(solution)/shard_map/concatenate | solution.py:480
  5.3 1.1 %copy.24 = bf16[768,64]{1,0:T(8,128)(2,1)S(1)} copy(bf16[768,64]{0,1:T(8,128)(2,1)} %param.14) | data formatting | bytes 196608 | tf_op args[4]
  6.4 1.1 %copy.25 = bf16[768,64]{1,0:T(8,128)(2,1)S(1)} copy(bf16[768,64]{0,1:T(8,128)(2,1)} %param.15) | data formatting | bytes 196608 | tf_op args[5]
  7.5 1.1 %copy.26 = bf16[768,64]{1,0:T(8,128)(2,1)S(1)} copy(bf16[768,64]{0,1:T(8,128)(2,1)} %param.16) | data formatting | bytes 196608 | tf_op args[6]
  8.5 0.9 %pad_maximum_fusion.wqkv = bf16[768,256]{1,0:T(8,128)(2,1)} fusion(bf16[768,64]{1,0:T(8,128)(2,1)S(1)} %copy.26, bf16[768,64]{1,0:T(8,128)(2,1)S(1)} %copy.25, bf16[768,64]{1,0:T(8,128)(2,1)S(1)} %copy.24, bf16[256]{0:T(256)(128)(2,1)S(1)} %pad.3.clone), kind=kLoop, calls=%fused_computation.4 | loop fusion | flops 1572864 | bytes 688640 | tf_op jit(solution)/shard_map/concatenate | solution.py:479
  9.5 0.0 copy-done
  9.5 0.2 reshape.19
  9.7 0.1 copy.23
  9.8 0.6 copy.32
  10.4 67.3 %shard_map.137 = (bf16[2,768,128]{2,1,0:T(8,128)(2,1)}, f32[8,128]{1,0:T(8,128)}) custom-call(bf16[1024,768]{1,0:T(8,128)(2,1)} %tiles.1, s32[1,1024]{1,0:T(1,128)} %bitcast.17, s32[1]{0:T(128)S(6)} %copy.33.counts, s32[2,1]{1,0:T(2,128)} %copy.27.offsets, bf16[768,256]{1,0:T(8,128)(2,1)} %pad_maximum_fusion.wqkv, bf16[64,768]{1,0:T(8,128)(2,1)} %w_out.1, ...), custom_call_target="tpu_custom_call" | custom-call | tf_op jit(solution)/shard_map/pallas_call | solution.py:505
  77.7 1.2 %slice.15 = f32[1,1]{1,0:T(1,128)} slice(f32[8,128]{1,0:T(8,128)} %get-tuple-element.7), slice={[0:1], [0:1]} | slice | bytes 8 | tf_op jit(solution)/shard_map/slice | solution.py:520
  78.8 1.0 %convert_element_type.3 = f32[2,768,128]{2,1,0:T(8,128)S(1)} convert(bf16[2,768,128]{2,1,0:T(8,128)(2,1)} %get-tuple-element.8) | non-fusion elementwise | flops 196608 | bytes 1179648 | tf_op jit(solution)/shard_map/convert_element_type | solution.py:518
  79.9 0.3 slice_bitcast_fusion
  80.2 0.8 copy.31
  81.0 0.8 copy.30
  81.8 0.8 copy.29
  82.7 0.8 copy.28
  (1 shorter events, 0.0 us)
Async XLA Ops:
  0.6 8.8 %copy-start = (s32[1024]{0:T(1024)S(1)}, s32[1024]{0:T(1024)}, u32[]{:S(2)}) copy-start(s32[1024]{0:T(1024)} %param.11) | copy-start | bytes 12292

commit v2 on v1

--- a/solution.py
+++ b/solution.py
@@ -44,9 +44,9 @@
 
 def kernel(
     dims,
-    tiles, labels, counts, offsets, wqkv, w_out, gain, wcc,
+    tiles, labels, counts, offsets, w_query, w_key, w_value, w_out, gain, w_class,
     res, loss_out,
-    xt, qs, kvs, ka0, va0, kv_all, ka2, va2, pr, ka1, va1, att_pk, wo,
+    wqkv, wcc, xt, qs, kvs, ka0, va0, kv_all, ka2, va2, pr, ka1, va1, att_pk, wo,
     acc0, m0, acc1, m1, qa, doa, atb, dmix, dq, dqp, dkv, dkvp,
     rs_out, rs_sib, rs_mid, rs_z, pr_out, pr_in, lt, ltz,
     pan, pan_sib, pan_half, pan_z,
@@ -92,11 +92,18 @@
     residues = [(c % sub_count) * ps + c // sub_count for c in range(fs)]
     count = counts[0]
     o1 = offsets[0, 0]
-    o2 = offsets[1, 0]
+    o2 = offsets[0, 1]
     c2 = lax.rem(o2, ps) * sub_count + lax.div(o2, ps)
 
     def rows_of(c):
         return pl.ds(c * far, far)
+
+    wqkv[pl.ds(0, hs), :] = w_query[...]
+    wqkv[pl.ds(hs, hs), :] = jnp.zeros((hs, d), BF16)
+    wqkv[pl.ds(2 * hs, hs), :] = w_key[...]
+    wqkv[pl.ds(3 * hs, hs), :] = w_value[...]
+    narrow = w_class[...].astype(F32)
+    wcc[...] = jnp.concatenate([narrow, narrow], axis=0).astype(BF16)
 
     per = PERM // fs
     a = lax.broadcasted_iota(jnp.int32, (PERM, PERM), 0)
@@ -107,7 +114,7 @@
     perm = (want == b).astype(F32).astype(BF16)
     for blk in range(n // PERM):
         moved = nn(perm, tiles[pl.ds(blk * PERM, PERM), :]).astype(BF16)
-        qkv = nn(moved, wqkv[...])
+        qkv = nt(moved, wqkv[...])
         q_part = (qkv[:, :128] * (1.0 / math.sqrt(hs))).astype(BF16)
         kv_part = qkv[:, 128:].astype(BF16)
         for c in range(fs):
@@ -174,7 +181,7 @@
         return top, nn(jnp.exp(s - top).astype(BF16), value)
 
     own_count = count.astype(F32)
-    step = min(256, far)
+    step = min(256, far // 2)
     for c in range(fs):
         key, value = augment(kvs[rows_of(c), :], subs(far) * fs + residues[c], own_count)
         ka0[rows_of(c), :] = key
@@ -244,29 +251,31 @@
         one, two, rest = three(-(top + jnp.log(total)))
         aux = jnp.where(lane == hs, 1.0, jnp.where(lane == hs + 1, one, jnp.where(lane == hs + 2, two, jnp.where(lane == hs + 3, rest, 0.0))))
         qa[rows, :] = jnp.where(lane < hs, qs[rows, :].astype(F32), aux).astype(BF16)
-    mid = n // 2
-    att_pk[0, :, :] = (
-        atb[pl.ds(0, mid), :].astype(F32) + pltpu.roll(atb[pl.ds(mid, mid), :].astype(F32), hs, 1)
-    ).astype(BF16)
-    for dh in range(1, nh):
-        att_c[dh] = push(att_pk.at[0], att_pk.at[dh], s_att.at[dh], r_att.at[dh], at_h(dh))
+        both = pltpu.roll(att, hs, 1)[far // 2:, :] + att[:far // 2, :]
+        att_pk[0, c] = both.astype(BF16)
+        for dh in range(1, nh):
+            att_c[c, dh] = push(att_pk.at[0, c], att_pk.at[dh, c], s_att.at[c, dh], r_att.at[c, dh], at_h(dh))
     for dh in range(1, nh):
         w_c[dh].wait_recv()
-    for dh in range(1, nh):
-        att_c[dh].wait_recv()
 
     loss = jnp.zeros((1, 1), F32)
-    g = gain[...]
+    g = gain[...].reshape(1, d)
+    span = step * fs
+    marks = labels[...].reshape(1, n).astype(F32)
+    pick_row = lax.broadcasted_iota(jnp.int32, (step, span), 0) * fs
+    pick_col = lax.broadcasted_iota(jnp.int32, (step, span), 1)
     for i in range(n // step):
         start = i * step
         c, inner = start // far, start % far
         rows = pl.ds(start, step)
         mixed = xt[rows, :].astype(F32)
         for dh in range(nh):
-            if start < mid:
-                term = nn(att_pk[dh, pl.ds(start, step), :], wo[dh, pl.ds(0, 2 * hs), :])
+            if dh and inner == 0:
+                att_c[c, dh].wait_recv()
+            if inner < far // 2:
+                term = nn(att_pk[dh, c, pl.ds(inner, step), :], wo[dh, pl.ds(0, 2 * hs), :])
             else:
-                term = nn(att_pk[dh, pl.ds(start - mid, step), :], wo[dh, pl.ds(hs, 2 * hs), :])
+                term = nn(att_pk[dh, c, pl.ds(inner - far // 2, step), :], wo[dh, pl.ds(hs, 2 * hs), :])
             mixed = mixed + term.astype(BF16).astype(F32)
         center = mixed - jnp.mean(mixed, axis=-1, keepdims=True)
         inv_dev = lax.rsqrt(jnp.mean(center * center, axis=-1, keepdims=True) + 1e-05)
@@ -275,8 +284,10 @@
         logits = nt(wcc[...], normed)[:classes, :]
         peak = jnp.max(logits, axis=0, keepdims=True)
         log_total = jnp.log(jnp.sum(jnp.exp(logits - peak), axis=0, keepdims=True)) + peak
-        kind = lax.broadcasted_iota(jnp.int32, (classes, step), 0)
-        onehot = (kind == labels[:, pl.ds(start, step)]).astype(F32)
+        kind = lax.broadcasted_iota(jnp.int32, (classes, step), 0).astype(F32)
+        chosen = (pick_row + residues[c] == pick_col).astype(F32).astype(BF16)
+        block = jnp.broadcast_to(marks[:, inner * fs:inner * fs + span], (classes, span)).astype(BF16)
+        onehot = (kind == nt(block, chosen)).astype(F32)
         spot = lax.broadcasted_iota(jnp.int32, (1, step), 1)
         ok = ((spot + inner) * fs + residues[c] < count).astype(F32)
         cross = log_total - jnp.sum(onehot * logits, axis=0, keepdims=True)
@@ -384,7 +395,8 @@
     first, second, third, fourth = {}, {}, {}, {}
 
     def start_panel(k, panel):
-        pan[k, pl.ds(0, d), :] = panel.astype(BF16)
+        for j in range(d // 128):
+            pan[k, pl.ds(j * 128, 128), :] = panel[:, j * 128:(j + 1) * 128].astype(BF16)
         if quarter * ps > d:
             pan[k, pl.ds(d, quarter * ps - d), :] = jnp.zeros((quarter * ps - d, 128), BF16)
         for dp in range(1, ps):
@@ -420,23 +432,28 @@
             third[k, dz] = push(
                 res.at[k, spot, :], res.at[k, spot, :], s_a3.at[k, dz], r_a3.at[k, dz], at_z(dz)
             )
+        share(k, 0)
+
+    def share(k, dz):
+        spot = pl.ds(pl.multiple_of(p * quarter + lax.rem(z + ns - dz, ns) * piece, 16), piece)
+        for dp in range(1, ps):
+            fourth[k, dz, dp] = push(
+                res.at[k, spot, :], res.at[k, spot, :], s_a4.at[k, dz, dp], r_a4.at[k, dz, dp], at_p(dp)
+            )
 
     def fourth_panel(k):
         for dz in range(1, ns):
             third[k, dz].wait_recv()
-        spot = pl.ds(pl.multiple_of(p * quarter, 16), quarter)
-        for dp in range(1, ps):
-            fourth[k, dp] = push(
-                res.at[k, spot, :], res.at[k, spot, :], s_a4.at[k, dp], r_a4.at[k, dp], at_p(dp)
-            )
-
-    start_panel(0, tn(xt[...], qa[...]) + tn(dmix[...], atb[...]))
+            share(k, dz)
+
+    start_panel(0, tn(qa[...], xt[...]) + tn(atb[...], dmix[...]))
 
     half_sum = dkvp[...]
     for dp in range(1, ps):
         pb_c[dp].wait_recv()
         half_sum = half_sum + pr_in[dp].astype(F32)
     dkvp[...] = half_sum
+    second_panel(0)
     for dz in range(1, ns):
         rz_c[dz].wait_recv()
         own_far = own_far + rs_z[dz].astype(F32)
@@ -447,8 +464,7 @@
         part = part + jnp.where(o1 == c // sub_count, dkvp[in_half, :], 0.0)
         part = part + jnp.where(c2 == c, own_far, 0.0)
         doa[rows, :] = part.astype(BF16)
-    second_panel(0)
-    start_panel(1, tn(xt[...], doa[...]))
+    start_panel(1, tn(doa[...], xt[...]))
     third_panel(0)
     second_panel(1)
     fourth_panel(0)
@@ -460,10 +476,21 @@
     loss_out[...] = total
     fourth_panel(1)
     for k in range(2):
-        for dp in range(1, ps):
-            fourth[k, dp].wait_recv()
+        for dz in range(ns):
+            for dp in range(1, ps):
+                fourth[k, dz, dp].wait_recv()
     for copy in sends:
         copy.wait_send()
+
+
+def unpack(hs, res, loss, tile_loss, g_query, g_key, g_value, g_out):
+    tile_loss[0] = loss[0, 0]
+    for j in range(g_query.shape[1] // 128):
+        cols = pl.ds(j * 128, 128)
+        g_query[:, cols] = res[0, pl.ds(j * 128, hs), :].astype(F32)
+        g_out[:, cols] = res[0, pl.ds(j * 128 + hs, hs), :].astype(F32)
+        g_key[:, cols] = res[1, pl.ds(j * 128, hs), :].astype(F32)
+        g_value[:, cols] = res[1, pl.ds(j * 128 + hs, hs), :].astype(F32)
 
 
 def body(ns, nh, ps, tiles, labels, counts, offsets, w_query, w_key, w_value, w_out, ln_gain, w_class):
@@ -475,18 +502,16 @@
     far, half = n // fs, n // ps
     piece = -(-d // (shards * 16)) * 16
     quarter = ns * piece
-    labels_row = labels.reshape(far, fs // ps, ps).transpose(2, 1, 0).reshape(1, n)
-    wqkv = jnp.concatenate([w_query, jnp.zeros((d, 128 - hs), BF16), w_key, w_value], axis=1)
-    wcc = jnp.concatenate([w_class.T, w_class.T], axis=0)
     vmem = pltpu.VMEM
     dma = lambda *shape: pltpu.SemaphoreType.DMA(shape)
     scratch = [
+        vmem((4 * hs, d), BF16), vmem((2 * classes, d), BF16),
         vmem((n, d), BF16), vmem((n, 128), BF16), vmem((n, 128), BF16),
         vmem((n, 128), BF16), vmem((n, 128), BF16),
         vmem((ns, ps, far + TAIL, 128), BF16),
         vmem((shards, far, 128), BF16), vmem((shards, far, 128), BF16),
         vmem((ps, half + TAIL, 128), BF16), vmem((n, 128), BF16), vmem((n, 128), BF16),
-        vmem((nh, n // 2, 128), BF16), vmem((nh, 3 * hs, d), BF16),
+        vmem((nh, fs, far // 2, 128), BF16), vmem((nh, 3 * hs, d), BF16),
         vmem((n, 128), F32), vmem((n, 128), F32), vmem((half, 128), F32), vmem((half, 128), F32),
         vmem((n, 128), BF16), vmem((n, 128), BF16), vmem((n, 128), BF16), vmem((n, d), BF16),
         vmem((n, 128), F32), vmem((half, 128), F32), vmem((n, 128), F32), vmem((half, 128), F32),
@@ -496,9 +521,9 @@
         vmem((ps, 8, 128), F32), vmem((ns, 8, 128), F32),
         vmem((2, ps * quarter, 128), BF16), vmem((2, ps, quarter, 128), BF16),
         vmem((2, quarter, 128), BF16), vmem((2, ns, piece, 128), BF16),
-        dma(ns), dma(ns), dma(ns, ps), dma(ns, ps), dma(ps), dma(ps), dma(nh), dma(nh), dma(nh), dma(nh),
+        dma(ns), dma(ns), dma(ns, ps), dma(ns, ps), dma(ps), dma(ps), dma(nh), dma(nh), dma(fs, nh), dma(fs, nh),
         dma(ns, ps), dma(ns, ps), dma(ns), dma(ns), dma(ps), dma(ps), dma(ps), dma(ps), dma(ns), dma(ns),
-        dma(2, ps), dma(2, ps), dma(2, ns), dma(2, ns), dma(2, ns), dma(2, ns), dma(2, ps), dma(2, ps),
+        dma(2, ps), dma(2, ps), dma(2, ns), dma(2, ns), dma(2, ns), dma(2, ns), dma(2, ns, ps), dma(2, ns, ps),
     ]
     whole = pl.BlockSpec(memory_space=pltpu.VMEM)
     scalar = pl.BlockSpec(memory_space=pltpu.SMEM)
@@ -508,17 +533,21 @@
             jax.ShapeDtypeStruct((2, ps * quarter, 128), BF16),
             jax.ShapeDtypeStruct((8, 128), F32),
         ),
-        in_specs=[whole, whole, scalar, scalar, whole, whole, whole, whole],
+        in_specs=[whole, whole, scalar, scalar] + [whole] * 6,
         out_specs=(whole, whole),
         scratch_shapes=scratch,
         compiler_params=pltpu.CompilerParams(
             collective_id=0, has_side_effects=True, vmem_limit_bytes=56 * 1024 * 1024
         ),
-    )(tiles, labels_row, counts, offsets, wqkv, w_out, ln_gain.reshape(1, d), wcc)
-    wide = res[:, :d, :].astype(F32)
-    return (
-        loss[0, :1], wide[0, :, :hs], wide[1, :, :hs], wide[1, :, hs:], wide[0, :, hs:].T,
-    )
+    )(tiles, labels, counts, offsets.T, w_query.T, w_key.T, w_value.T, w_out, ln_gain, w_class.T)
+    flat = jax.ShapeDtypeStruct((hs, d), F32)
+    tile_loss, g_query, g_key, g_value, g_out = pl.pallas_call(
+        functools.partial(unpack, hs),
+        out_shape=(jax.ShapeDtypeStruct((1,), F32), flat, flat, flat, flat),
+        in_specs=[whole, whole],
+        out_specs=(scalar, whole, whole, whole, whole),
+    )(res, loss)
+    return (tile_loss, g_query.T, g_key.T, g_value.T, g_out)
 
 
 def solution(mesh):

time: 83.9 us -> 69.2 us (0.82)
  local copies, waits for them, and re-layouts: 11.5 us -> 0 us
  other arithmetic: 3.36 us -> 0 us
    unnamed x11 -> x0, local copies, waits for them, and re-layouts: 8.4 us -> none
    concatenate x2 -> x0, other arithmetic: 2.32 us -> none  [the longest x1 1.39 us: body(): wcc = jnp.concatenate([w_class.T, w_class.T], axis=0)]
    pallas_call x0 -> x1, Pallas kernels: none -> 1.89 us  [body(): pl.pallas_call(functools.partial(unpack, hs), out_shape=(jax.ShapeDtypeSt...]
    pallas_call x1, Pallas kernels: 67.3 us -> 65.6 us  [body(): pl.pallas_call(functools.partial(kernel, (ns, nh, ps, fs, hs, classes, pi...]
    reshape x2 -> x0, local copies, waits for them, and re-layouts: 1.46 us -> none  [the longest x1 1.27 us: body(): ln_gain.reshape(1, d)]
    slice x1 -> x0, local copies, waits for them, and re-layouts: 1.19 us -> none  [body(): loss[0, :1]]
    convert_element_type x1 -> x0, other arithmetic: 1.05 us -> none  [body(): wide = res[:, :d, :].astype(F32)]
where the time goes in v2:
time: 69.2 us; the launch traced here: 69 us
  Pallas kernels  67.5 us (98%)
  between operations  1.47 us (2%)
    pallas_call x1, Pallas kernels, body(): pl.pallas_call(functools.partial(kernel, (ns, nh, ps, fs, hs, classes, pi...  65.6 us
    pallas_call x1, Pallas kernels, body(): pl.pallas_call(functools.partial(unpack, hs), out_shape=(jax.ShapeDtypeSt...  1.89 us

profile of v2, /device:TPU:0, one launch (start us, length us, event | category | flops | bytes accessed | tf_op | source)
XLA Modules:
  0.0 69.0 jit_solution(15194926222146385865)
XLA Ops:
  1.3 65.6 %shard_map.137 = (bf16[2,768,128]{2,1,0:T(8,128)(2,1)}, f32[8,128]{1,0:T(8,128)}) custom-call(bf16[1024,768]{1,0:T(8,128)(2,1)} %tiles.1, s32[1024]{0:T(1024)} %labels.1, s32[1]{0:T(128)S(6)} %copy.15.counts, s32[1,2]{1,0:T(1,128)} %bitcast.12, bf16[64,768]{1,0:T(8,128)(2,1)} %bitcast.8, bf16[64,768]{1,0:T(8,128)(2,1)} %bitcast.9, bf16[64,768]{1,0:T(8,128)(2,1)} %bitcast.10, ...), custom_call_target="tpu_custom_call" | custom-call | tf_op jit(solution)/shard_map/pallas_call | solution.py:530
  66.9 1.9 %shard_map.138 = (f32[1]{0:T(128)}, f32[64,768]{1,0:T(8,128)}, f32[64,768]{1,0:T(8,128)}, f32[64,768]{1,0:T(8,128)}, f32[64,768]{1,0:T(8,128)}) custom-call(bf16[2,768,128]{2,1,0:T(8,128)(2,1)} %get-tuple-element.12.res, f32[8,128]{1,0:T(8,128)} %get-tuple-element.13.loss), custom_call_target="tpu_custom_call" | custom-call | tf_op jit(solution)/shard_map/pallas_call | solution.py:544

commit v3 on v2

--- a/solution.py
+++ b/solution.py
@@ -63,6 +63,14 @@
     def at_z(dz):
         return {"seq": lax.rem(z + dz, ns)}
 
+    def at_x(e):
+        place, bit = z, 1
+        while bit < ns:
+            if e & bit:
+                place = place + bit - 2 * bit * lax.rem(lax.div(z, bit), 2)
+            bit *= 2
+        return {"seq": place}
+
     def at_p(dp):
         return {"rep": lax.rem(p + dp, ps)}
 
@@ -148,8 +156,8 @@
 
     pl.semaphore_wait(barrier, len(peers))
     far_z = {}
-    for dz in range(1, ns):
-        far_z[dz] = push(kv_all.at[0, 0], kv_all.at[dz, 0], s_far.at[dz], r_far.at[dz], at_z(dz))
+    for e in list(range(2, ns, 2)) + [1]:
+        far_z[e] = push(kv_all.at[0, 0], kv_all.at[e, 0], s_far.at[e], r_far.at[e], at_x(e))
     pr_c, fwd_c, w_c, att_c = {}, {}, {}, {}
     for dp in range(1, ps):
         pr_c[dp] = push(pr.at[0], pr.at[dp], s_pr.at[dp], r_pr.at[dp], at_p(dp))
@@ -209,32 +217,45 @@
         acc1[spot, :] = acc
 
     q_far = with_one(pick_far(qs))
-    order = [(0, dp) for dp in range(ps)]
-    for dz in range(1, ns):
-        order += [(dz, dp) for dp in range(ps)]
-    top2 = acc2 = None
-    for dz in range(1, ns):
-        far_z[dz].wait_recv()
+    running = [None, None]
+
+    def arrived(e):
+        far_z[e].wait_recv()
+        if e and e % 2 == 0:
+            far_z[e + 1] = push(
+                kv_all.at[e, 0], kv_all.at[e + 1, 0], s_far.at[e + 1], r_far.at[e + 1], at_x(1)
+            )
         for dp in range(1, ps):
-            fwd_c[dz, dp] = push(
-                kv_all.at[dz, 0], kv_all.at[dz, dp], s_fwd.at[dz, dp], r_fwd.at[dz, dp], at_p(dp)
+            fwd_c[e, dp] = push(
+                kv_all.at[e, 0], kv_all.at[e, dp], s_fwd.at[e, dp], r_fwd.at[e, dp], at_p(dp)
             )
-        for bz, dp in [(dz - 1, i) for i in range(ps)] + ([(dz, i) for i in range(ps)] if dz == ns - 1 else []):
+
+    def use(e):
+        for dp in range(ps):
             if dp:
-                fwd_c[bz, dp].wait_recv()
+                fwd_c[e, dp].wait_recv()
             key, value = augment(
-                kv_all[bz, dp, pl.ds(0, far), :], subs(far) * fs + o2,
-                remote_count(kv_all[bz, dp, pl.ds(far, TAIL), :]),
+                kv_all[e, dp, pl.ds(0, far), :], subs(far) * fs + o2,
+                remote_count(kv_all[e, dp, pl.ds(far, TAIL), :]),
             )
-            ka2[bz * ps + dp] = key
-            va2[bz * ps + dp] = value
+            ka2[e * ps + dp] = key
+            va2[e * ps + dp] = value
             top, acc = forward(q_far, key, value)
-            if top2 is None:
-                top2, acc2 = top, acc
-            else:
-                both = jnp.maximum(top, top2)
-                acc2 = acc2 * jnp.exp(top2 - both) + acc * jnp.exp(top - both)
-                top2 = both
+            if running[0] is not None:
+                both = jnp.maximum(top, running[0])
+                acc = running[1] * jnp.exp(running[0] - both) + acc * jnp.exp(top - both)
+                top = both
+            running[:] = [top, acc]
+
+    arrived(1)
+    use(0)
+    for e in range(2, ns, 2):
+        arrived(e)
+        use(e - 1)
+        use(e)
+        arrived(e + 1)
+    use(ns - 1)
+    top2, acc2 = running
 
     for c in range(fs):
         rows = rows_of(c)
@@ -322,30 +343,37 @@
     q_far = pick_far(qa).astype(BF16)
     do_far = pick_far(doa).astype(BF16)
     dq_far = None
-    rz_c = {}
-    own_far = None
-    for dz in list(range(1, ns)) + [0]:
-        rs_c = {}
-        own = None
+    rz_c, rs_c, own = {}, {}, {}
+
+    def settle(e):
+        total = own[e]
+        for dp in range(1, ps):
+            rs_c[e, dp].wait_recv()
+            total = total + rs_sib[e, dp].astype(F32)
+        own[e] = total
+        if e % 2:
+            rs_mid[e] = total.astype(BF16)
+            rz_c[e] = push(rs_mid.at[e], rs_z.at[e], s_rz.at[e], r_rz.at[e], at_x(1))
+
+    turns = list(range(3, ns, 2)) + list(range(2, ns, 2)) + [1, 0]
+    for turn, e in enumerate(turns):
         for dp in list(range(1, ps)) + [0]:
-            key_rows = dz * ps + dp
+            if dp == 0 and turn:
+                settle(turns[turn - 1])
+            key_rows = e * ps + dp
             d_q, d_kv = backward(q_far, do_far, ka2[key_rows], va2[key_rows])
             dq_far = d_q if dq_far is None else dq_far + d_q
             if dp:
-                rs_out[dz, dp] = d_kv.astype(BF16)
-                rs_c[dp] = push(
-                    rs_out.at[dz, dp], rs_sib.at[dz, dp], s_rs.at[dz, dp], r_rs.at[dz, dp], at_p(ps - dp)
+                rs_out[e, dp] = d_kv.astype(BF16)
+                rs_c[e, dp] = push(
+                    rs_out.at[e, dp], rs_sib.at[e, dp], s_rs.at[e, dp], r_rs.at[e, dp], at_p(ps - dp)
                 )
             else:
-                own = d_kv
-        for dp in range(1, ps):
-            rs_c[dp].wait_recv()
-            own = own + rs_sib[dz, dp].astype(F32)
-        if dz:
-            rs_mid[dz] = own.astype(BF16)
-            rz_c[dz] = push(rs_mid.at[dz], rs_z.at[dz], s_rz.at[dz], r_rz.at[dz], at_z(ns - dz))
-        else:
-            own_far = own
+                own[e] = d_kv
+    for e in range(2, ns, 2):
+        rz_c[e + 1].wait_recv()
+        rs_mid[e] = (own[e] + rs_z[e + 1].astype(F32)).astype(BF16)
+        rz_c[e] = push(rs_mid.at[e], rs_z.at[e], s_rz.at[e], r_rz.at[e], at_x(e))
 
     whole_loss = lt[0, :, :]
     for dp in range(1, ps):
@@ -454,9 +482,11 @@
         half_sum = half_sum + pr_in[dp].astype(F32)
     dkvp[...] = half_sum
     second_panel(0)
-    for dz in range(1, ns):
-        rz_c[dz].wait_recv()
-        own_far = own_far + rs_z[dz].astype(F32)
+    settle(0)
+    own_far = own[0]
+    for e in [1] + list(range(2, ns, 2)):
+        rz_c[e].wait_recv()
+        own_far = own_far + rs_z[e].astype(F32)
     for c in range(fs):
         rows = rows_of(c)
         in_half = pl.ds((c % sub_count) * far, far)

time: 69.2 us -> 65.9 us (0.952)
  Pallas kernels: 67.5 us -> 64.2 us
    pallas_call x1, Pallas kernels: 65.6 us -> 62.3 us  [body(): pl.pallas_call(functools.partial(kernel, (ns, nh, ps, fs, hs, classes, pi...]
where the time goes in v3:
time: 65.9 us; the launch traced here: 65.7 us
  Pallas kernels  64.2 us (97%)
  between operations  1.47 us (2%)
    pallas_call x1, Pallas kernels, body(): pl.pallas_call(functools.partial(kernel, (ns, nh, ps, fs, hs, classes, pi...  62.3 us
    pallas_call x1, Pallas kernels, body(): pl.pallas_call(functools.partial(unpack, hs), out_shape=(jax.ShapeDtypeSt...  1.89 us

profile of v3, /device:TPU:0, one launch (start us, length us, event | category | flops | bytes accessed | tf_op | source)
XLA Modules:
  0.0 65.7 jit_solution(6159962140614517960)
XLA Ops:
  1.3 62.3 %shard_map.137 = (bf16[2,768,128]{2,1,0:T(8,128)(2,1)}, f32[8,128]{1,0:T(8,128)}) custom-call(bf16[1024,768]{1,0:T(8,128)(2,1)} %tiles.1, s32[1024]{0:T(1024)} %labels.1, s32[1]{0:T(128)S(6)} %copy.15.counts, s32[1,2]{1,0:T(1,128)} %bitcast.12, bf16[64,768]{1,0:T(8,128)(2,1)} %bitcast.8, bf16[64,768]{1,0:T(8,128)(2,1)} %bitcast.9, bf16[64,768]{1,0:T(8,128)(2,1)} %bitcast.10, ...), custom_call_target="tpu_custom_call" | custom-call | tf_op jit(solution)/shard_map/pallas_call | solution.py:560
  63.6 1.9 %shard_map.138 = (f32[1]{0:T(128)}, f32[64,768]{1,0:T(8,128)}, f32[64,768]{1,0:T(8,128)}, f32[64,768]{1,0:T(8,128)}, f32[64,768]{1,0:T(8,128)}) custom-call(bf16[2,768,128]{2,1,0:T(8,128)(2,1)} %get-tuple-element.12.res, f32[8,128]{1,0:T(8,128)} %get-tuple-element.13.loss), custom_call_target="tpu_custom_call" | custom-call | tf_op jit(solution)/shard_map/pallas_call | solution.py:574

commit v4 on v3

--- a/solution.py
+++ b/solution.py
@@ -156,8 +156,17 @@
 
     pl.semaphore_wait(barrier, len(peers))
     far_z = {}
+    parts = (pl.ds(0, far // 2), pl.ds(far // 2, far // 2 + TAIL))
+
+    def far_push(held, e, k, where):
+        far_z[e, k] = push(
+            kv_all.at[held, 0, parts[k], :], kv_all.at[e, 0, parts[k], :],
+            s_far.at[e, k], r_far.at[e, k], where,
+        )
+
     for e in list(range(2, ns, 2)) + [1]:
-        far_z[e] = push(kv_all.at[0, 0], kv_all.at[e, 0], s_far.at[e], r_far.at[e], at_x(e))
+        for k in range(2):
+            far_push(0, e, k, at_x(e))
     pr_c, fwd_c, w_c, att_c = {}, {}, {}, {}
     for dp in range(1, ps):
         pr_c[dp] = push(pr.at[0], pr.at[dp], s_pr.at[dp], r_pr.at[dp], at_p(dp))
@@ -219,16 +228,20 @@
     q_far = with_one(pick_far(qs))
     running = [None, None]
 
-    def arrived(e):
-        far_z[e].wait_recv()
-        if e and e % 2 == 0:
-            far_z[e + 1] = push(
-                kv_all.at[e, 0], kv_all.at[e + 1, 0], s_far.at[e + 1], r_far.at[e + 1], at_x(1)
-            )
+    def relay(e, k):
+        far_z[e, k].wait_recv()
+        far_push(e, e + 1, k, at_x(1))
+
+    def share_far(e):
         for dp in range(1, ps):
             fwd_c[e, dp] = push(
                 kv_all.at[e, 0], kv_all.at[e, dp], s_fwd.at[e, dp], r_fwd.at[e, dp], at_p(dp)
             )
+
+    def arrived(e):
+        for k in range(2):
+            far_z[e, k].wait_recv()
+        share_far(e)
 
     def use(e):
         for dp in range(ps):
@@ -247,13 +260,16 @@
                 top = both
             running[:] = [top, acc]
 
-    arrived(1)
-    use(0)
     for e in range(2, ns, 2):
-        arrived(e)
+        relay(e, 0)
+        if e == 2:
+            use(0)
+        relay(e, 1)
+        share_far(e)
+        arrived(e - 1)
         use(e - 1)
         use(e)
-        arrived(e + 1)
+    arrived(ns - 1)
     use(ns - 1)
     top2, acc2 = running
 
@@ -370,11 +386,6 @@
                 )
             else:
                 own[e] = d_kv
-    for e in range(2, ns, 2):
-        rz_c[e + 1].wait_recv()
-        rs_mid[e] = (own[e] + rs_z[e + 1].astype(F32)).astype(BF16)
-        rz_c[e] = push(rs_mid.at[e], rs_z.at[e], s_rz.at[e], r_rz.at[e], at_x(e))
-
     whole_loss = lt[0, :, :]
     for dp in range(1, ps):
         lt_c[dp].wait_recv()
@@ -397,6 +408,11 @@
             dkvp[...] = d_kv
     dqp[...] = dq_half
 
+    for e in range(2, ns, 2):
+        rz_c[e + 1].wait_recv()
+        rs_mid[e] = (own[e] + rs_z[e + 1].astype(F32)).astype(BF16)
+        rz_c[e] = push(rs_mid.at[e], rs_z.at[e], s_rz.at[e], r_rz.at[e], at_x(e))
+
     tile = min(512, n)
     for j in range(n // tile):
         key_rows = pl.ds(j * tile, tile)
@@ -482,19 +498,20 @@
         half_sum = half_sum + pr_in[dp].astype(F32)
     dkvp[...] = half_sum
     second_panel(0)
+    for c in range(fs):
+        rows = rows_of(c)
+        in_half = pl.ds((c % sub_count) * far, far)
+        part = dkv[rows, :] + jnp.where(o1 == c // sub_count, dkvp[in_half, :], 0.0)
+        dkv[rows, :] = part
+        doa[rows, :] = jnp.where(c2 == c, 0.0, part).astype(BF16)
+    near = tn(doa[...], xt[...])
+    xt_far = pick_far(xt).astype(BF16)
     settle(0)
-    own_far = own[0]
+    own_far = own[0] + pick_far(dkv)
     for e in [1] + list(range(2, ns, 2)):
         rz_c[e].wait_recv()
         own_far = own_far + rs_z[e].astype(F32)
-    for c in range(fs):
-        rows = rows_of(c)
-        in_half = pl.ds((c % sub_count) * far, far)
-        part = dkv[rows, :]
-        part = part + jnp.where(o1 == c // sub_count, dkvp[in_half, :], 0.0)
-        part = part + jnp.where(c2 == c, own_far, 0.0)
-        doa[rows, :] = part.astype(BF16)
-    start_panel(1, tn(doa[...], xt[...]))
+    start_panel(1, near + tn(own_far.astype(BF16), xt_far))
     third_panel(0)
     second_panel(1)
     fourth_panel(0)
@@ -551,7 +568,7 @@
         vmem((ps, 8, 128), F32), vmem((ns, 8, 128), F32),
         vmem((2, ps * quarter, 128), BF16), vmem((2, ps, quarter, 128), BF16),
         vmem((2, quarter, 128), BF16), vmem((2, ns, piece, 128), BF16),
-        dma(ns), dma(ns), dma(ns, ps), dma(ns, ps), dma(ps), dma(ps), dma(nh), dma(nh), dma(fs, nh), dma(fs, nh),
+        dma(ns, 2), dma(ns, 2), dma(ns, ps), dma(ns, ps), dma(ps), dma(ps), dma(nh), dma(nh), dma(fs, nh), dma(fs, nh),
         dma(ns, ps), dma(ns, ps), dma(ns), dma(ns), dma(ps), dma(ps), dma(ps), dma(ps), dma(ns), dma(ns),
         dma(2, ps), dma(2, ps), dma(2, ns), dma(2, ns), dma(2, ns), dma(2, ns), dma(2, ns, ps), dma(2, ns, ps),
     ]

time: 65.9 us -> 65.7 us (level)
  no operation moved by 1% of the time
where the time goes in v4:
time: 65.7 us; the launch traced here: 65.6 us
  Pallas kernels  64.1 us (98%)
  between operations  1.47 us (2%)
    pallas_call x1, Pallas kernels, body(): pl.pallas_call(functools.partial(kernel, (ns, nh, ps, fs, hs, classes, pi...  62.2 us
    pallas_call x1, Pallas kernels, body(): pl.pallas_call(functools.partial(unpack, hs), out_shape=(jax.ShapeDtypeSt...  1.89 us

profile of v4, /device:TPU:0, one launch (start us, length us, event | category | flops | bytes accessed | tf_op | source)
XLA Modules:
  0.0 65.6 jit_solution(3629010451085212110)
XLA Ops:
  1.3 62.2 %shard_map.137 = (bf16[2,768,128]{2,1,0:T(8,128)(2,1)}, f32[8,128]{1,0:T(8,128)}) custom-call(bf16[1024,768]{1,0:T(8,128)(2,1)} %tiles.1, s32[1024]{0:T(1024)} %labels.1, s32[1]{0:T(128)S(6)} %copy.15.counts, s32[1,2]{1,0:T(1,128)} %bitcast.12, bf16[64,768]{1,0:T(8,128)(2,1)} %bitcast.8, bf16[64,768]{1,0:T(8,128)(2,1)} %bitcast.9, bf16[64,768]{1,0:T(8,128)(2,1)} %bitcast.10, ...), custom_call_target="tpu_custom_call" | custom-call | tf_op jit(solution)/shard_map/pallas_call | solution.py:577
  63.5 1.9 %shard_map.138 = (f32[1]{0:T(128)}, f32[64,768]{1,0:T(8,128)}, f32[64,768]{1,0:T(8,128)}, f32[64,768]{1,0:T(8,128)}, f32[64,768]{1,0:T(8,128)}) custom-call(bf16[2,768,128]{2,1,0:T(8,128)(2,1)} %get-tuple-element.12.res, f32[8,128]{1,0:T(8,128)} %get-tuple-element.13.loss), custom_call_target="tpu_custom_call" | custom-call | tf_op jit(solution)/shard_map/pallas_call | solution.py:591
